TPU v7x, 32 devices: a whole 2x2x4 slice. The times are simulated.
32 devices in a mesh: seq: 4 (over x, core), rows: 8 (over z, y).
Axes of the slice: x: 2, y: 2, z: 4, core: 2. Of those that a mesh axis runs over, the one named last changes fastest.
Arguments:
- inputs: bfloat16 [16, 2048, 768], P('rows', 'seq'), may hold values from -6 to 6
- query_weight: bfloat16 [768, 768], replicated, may hold values from -0.21875 to 0.21875
- query_bias: bfloat16 [768], replicated, may hold values from -1.5 to 1.5
- key_weight: bfloat16 [768, 768], replicated, may hold values from -0.21875 to 0.21875
- value_weight: bfloat16 [768, 768], replicated, may hold values from -0.21875 to 0.21875
- value_bias: bfloat16 [768], replicated, may hold values from -1.5 to 1.5
- output_weight: bfloat16 [768, 768], replicated, may hold values from -1.5 to 1.5
- output_bias: bfloat16 [768], replicated, may hold values from -1.5 to 1.5
- first_gain: bfloat16 [768], replicated, may hold values from 0.5 to 1.5
- first_shift: bfloat16 [768], replicated, may hold values from -1 to 1
- inner_weight: bfloat16 [768, 3072], replicated, may hold values from -0.21875 to 0.21875
- inner_bias: bfloat16 [3072], replicated, may hold values from -1.5 to 1.5
- outer_weight: bfloat16 [3072, 768], replicated, may hold values from -0.109375 to 0.109375
- outer_bias: bfloat16 [768], replicated, may hold values from -1.5 to 1.5
- second_gain: bfloat16 [768], replicated, may hold values from 0.5 to 1.5
- second_shift: bfloat16 [768], replicated, may hold values from -1 to 1
- doc_tokens: int32 [16], P('rows'), may hold values from 512 to 2048, as said below
- random_blocks: int32 [16, 32, 3], P('rows'), may hold values from 2 to 31, as said below
- cotangent: bfloat16 [16, 2048, 768], P('rows', 'seq'), may hold values from -6 to 6
Outputs:
- outputs: bfloat16 [16, 2048, 768], P('rows', 'seq')
- input_gradient: bfloat16 [16, 2048, 768], P('rows', 'seq')
- query_weight_gradient: float32 [768, 768], replicated
- query_bias_gradient: float32 [768], replicated
- key_weight_gradient: float32 [768, 768], replicated
- value_weight_gradient: float32 [768, 768], replicated
- value_bias_gradient: float32 [768], replicated
- output_weight_gradient: float32 [768, 768], replicated
- output_bias_gradient: float32 [768], replicated
- first_gain_gradient: float32 [768], replicated
- first_shift_gradient: float32 [768], replicated
- inner_weight_gradient: float32 [768, 3072], replicated
- inner_bias_gradient: float32 [3072], replicated
- outer_weight_gradient: float32 [3072, 768], replicated
- outer_bias_gradient: float32 [768], replicated
- second_gain_gradient: float32 [768], replicated
- second_shift_gradient: float32 [768], replicated
Inputs may be any that keep to these rules, and one draw needn't show every extreme that they name: `doc_tokens`: in each aligned block of 2 rows one row, drawn from the seed, holds a document of more than 1536 tokens; one row of the batch, drawn from the seed, holds exactly 2048. `random_blocks`: for query block i of a row the 3 entries are distinct, and none of them is 0, 1, i - 1, i or i + 1.
All inputs are finite; a program needn't handle non-finite values.
Results may differ from a plain program's by a relative error of at most 0.015.
Values may be sent and summed in bfloat16 or wider, within the bound.
No kernel may reach another device: no remote copies, remote signals or barrier semaphores. Data moves between devices by JAX's collectives and lax.ppermute only.
A program may use at most 512 MiB of HBM per device.

v0:
```python
import functools
from functools import partial

import jax
import jax.numpy as jnp
from jax import lax
from jax.experimental import pallas as pl
from jax.experimental.pallas import tpu as pltpu
from jax.sharding import PartitionSpec as P

D = 768
HEADS = 12
HEAD = 64
BLOCK = 64
SETS = 8
CHIPS_Z = 4

EPSILON = 1e-05
NEG_FILL = -1e30

SHORT = pl.CostEstimate(flops=1 << 20, bytes_accessed=1 << 10, transcendentals=0)

NT = (((1,), (1,)), ((), ()))
NN = (((1,), (0,)), ((), ()))
TN = (((0,), (0,)), ((), ()))


def dot(left, right, dims):
    return lax.dot_general(left, right, dims, preferred_element_type=jnp.float32)


def head_groups(heads):
    groups, at = [], 0
    while at < heads:
        n = 2 if heads - at >= 2 else 1
        groups.append((at, n))
        at += n
    return groups


def lanes_of(at, n):
    return slice(at * HEAD, (at + n) * HEAD)


def diagonal(n, rows):
    row = lax.broadcasted_iota(jnp.int32, (n * rows, n * HEAD), 0) // rows
    lane = lax.broadcasted_iota(jnp.int32, (n * rows, n * HEAD), 1) // HEAD
    return (row == lane).astype(jnp.float32)


def spread_heads(block, diag, n):
    if n == 1:
        return block
    return jnp.concatenate([block] * n, 0) * diag.astype(block.dtype)


def fold_heads(full, diag, n):
    if n == 1:
        return full
    rows = full.shape[0] // n
    kept = full * diag
    out = kept[:rows]
    for h in range(1, n):
        out = out + kept[h * rows : (h + 1) * rows]
    return out


def rows_of(slot):
    return pl.ds(pl.multiple_of(slot * BLOCK, BLOCK), BLOCK)


def gather_rows(ref, slots, lanes):
    return jnp.concatenate([ref[rows_of(s), lanes] for s in slots], 0)


def as_row(column):
    n = column.shape[0]
    same = lax.broadcasted_iota(jnp.int32, (n, n), 0) == lax.broadcasted_iota(jnp.int32, (n, n), 1)
    return jnp.sum(jnp.where(same, column, 0.0), 0, keepdims=True)


def attend_kernel(
    heads,
    nb,
    abreast,
    key_at_ref,
    query_at_ref,
    q_ref,
    k_ref,
    v_ref,
    task_bias_ref,
    lead_bias_ref,
    o_ref,
    lse_ref,
):
    groups = head_groups(heads)
    scale = jnp.bfloat16(HEAD**-0.5)
    diags = {n: diagonal(n, BLOCK) for _, n in groups}

    def local(i, carry):
        work, scores, probs = [], [], []
        for u in range(abreast):
            t = abreast * i + u
            ks = [key_at_ref[t, b] for b in range(SETS)]
            work += [(t, ks, query_at_ref[t], lanes_of(at, n), n) for at, n in groups]
        for t, ks, qs, lanes, n in work:
            query = spread_heads(q_ref[rows_of(qs), lanes] * scale, diags[n], n)
            score = dot(query, gather_rows(k_ref, ks, lanes), NT)
            scores.append(score + task_bias_ref[pl.ds(t, 1), :])
        for score in scores:
            top = jnp.max(score, 1, keepdims=True)
            prob = jnp.exp(score - top)
            probs.append((prob.astype(jnp.bfloat16), top, jnp.sum(prob, 1, keepdims=True)))
        for (t, ks, qs, lanes, n), (prob, top, total) in zip(work, probs):
            out = dot(prob, gather_rows(v_ref, ks, lanes), NN) * (1.0 / total)
            out = fold_heads(out, diags[n], n)
            o_ref[rows_of(qs), lanes] = out.astype(jnp.bfloat16)
            lse_ref[qs, :, lanes] = as_row(top + jnp.log(total))
        return carry

    lax.fori_loop(0, (nb - 2) // abreast, local, 0)

    rows = 2 * BLOCK
    qs = query_at_ref[nb - 2]
    lead_rows = pl.ds(pl.multiple_of(qs * BLOCK, BLOCK), rows)
    scores, probs = [], []
    for at, n in groups:
        lanes = lanes_of(at, n)
        query = spread_heads(q_ref[lead_rows, lanes] * scale, diagonal(n, rows), n)
        scores.append(dot(query, k_ref[:, lanes], NT) + lead_bias_ref[...])
    for score in scores:
        top = jnp.max(score, 1, keepdims=True)
        prob = jnp.exp(score - top)
        probs.append((prob.astype(jnp.bfloat16), top, jnp.sum(prob, 1, keepdims=True)))
    for (at, n), (prob, top, total) in zip(groups, probs):
        lanes = lanes_of(at, n)
        out = dot(prob, v_ref[:, lanes], NN) * (1.0 / total)
        o_ref[lead_rows, lanes] = fold_heads(out, diagonal(n, rows), n).astype(jnp.bfloat16)
        lse = top + jnp.log(total)
        each = [as_row(lse[h * rows : (h + 1) * rows]) for h in range(n)]
        for b in range(2):
            part = slice(b * BLOCK, (b + 1) * BLOCK)
            lse_ref[qs + b, :, lanes] = jnp.concatenate([row[:, part] for row in each], 1)


def attend_back_kernel(
    heads,
    nb,
    abreast,
    pieces,
    key_at_ref,
    bias_at_ref,
    query_at_ref,
    q_ref,
    k_ref,
    v_ref,
    o_ref,
    lse_ref,
    bias_ref,
    *rest,
):
    dq_ref, dk_ref, dv_ref, dk_acc, dv_acc, delta_ref, g_ref = rest[-7:]
    rows = nb * BLOCK // pieces
    for i in range(pieces):
        g_ref[i * rows : (i + 1) * rows, :] = rest[i][...]
    groups = head_groups(heads)
    diags = {n: diagonal(n, BLOCK) for _, n in groups}
    every = nb * BLOCK
    dk_acc[every:, :] = jnp.zeros_like(dk_acc[every:, :])
    dv_acc[every:, :] = jnp.zeros_like(dv_acc[every:, :])
    scale = HEAD**-0.5

    for at, n in groups:
        lanes = lanes_of(at, n)
        row = lax.broadcasted_iota(jnp.int32, (16, n * HEAD), 0)
        pick = row == lax.broadcasted_iota(jnp.int32, (16, n * HEAD), 1) // HEAD
        pick = pick.astype(jnp.float32).astype(jnp.bfloat16)
        for s in range(0, nb, 4):
            some = slice(s * BLOCK, (s + 4) * BLOCK)
            both = g_ref[some, lanes].astype(jnp.float32) * o_ref[some, lanes].astype(jnp.float32)
            high = both.astype(jnp.bfloat16)
            less = (both - high.astype(jnp.float32)).astype(jnp.bfloat16)
            delta = dot(pick, high, NT) + dot(pick, less, NT)
            for j in range(4):
                part = slice(j * BLOCK, (j + 1) * BLOCK)
                delta_ref[s + j, :, lanes] = jnp.concatenate(
                    [delta[h : h + 1, part] for h in range(n)], 1
                )

    both_rows = 2 * BLOCK
    lead = query_at_ref[nb - 2]
    lead_rows = pl.ds(pl.multiple_of(lead * BLOCK, BLOCK), both_rows)

    def lead_row(ref, lanes, n):
        first, second = ref[lead, :, lanes], ref[lead + 1, :, lanes]
        heads_of = [slice(h * HEAD, (h + 1) * HEAD) for h in range(n)]
        return jnp.concatenate([r[:, h] for h in heads_of for r in (first, second)], 1)

    for at, n in groups:
        lanes, diag = lanes_of(at, n), diagonal(n, both_rows)
        query = spread_heads(q_ref[lead_rows, lanes] * jnp.bfloat16(scale), diag, n)
        grad = spread_heads(g_ref[lead_rows, lanes], diag, n)
        score = dot(k_ref[:, lanes], query, NT)
        bias = jnp.concatenate([bias_ref[:every, :]] * n, 1)
        prob = jnp.exp(score + bias - lead_row(lse_ref, lanes, n))
        d_prob = dot(v_ref[:, lanes], grad, NT)
        d_score = (prob * (d_prob - lead_row(delta_ref, lanes, n))).astype(jnp.bfloat16)
        dv_acc[:every, lanes] = dot(prob.astype(jnp.bfloat16), grad, NN)
        dk_acc[:every, lanes] = dot(d_score, query, NN)
        d_query = fold_heads(dot(d_score, k_ref[:, lanes], TN), diag, n) * scale
        dq_ref[lead_rows, lanes] = d_query.astype(jnp.bfloat16)

    def several(i, carry):
        work, scores, probs, grads = [], [], [], []
        for u in range(abreast):
            t = abreast * i + u
            ks = [key_at_ref[t, b] for b in range(SETS)]
            bs = [bias_at_ref[t, b] for b in range(SETS)]
            work += [(ks, bs, query_at_ref[t], lanes_of(at, n), n) for at, n in groups]
        for ks, bs, qs, lanes, n in work:
            diag = diags[n]
            query = spread_heads(q_ref[rows_of(qs), lanes] * jnp.bfloat16(scale), diag, n)
            grad = spread_heads(g_ref[rows_of(qs), lanes], diag, n)
            keys = gather_rows(k_ref, ks, lanes)
            score = dot(keys, query, NT)
            d_prob = dot(gather_rows(v_ref, ks, lanes), grad, NT)
            scores.append((query, grad, keys, score, d_prob))
        for (ks, bs, qs, lanes, n), (query, grad, keys, score, d_prob) in zip(work, scores):
            bias = gather_rows(bias_ref, bs, slice(None))[:, : n * HEAD]
            prob = jnp.exp(score + bias - lse_ref[qs, :, lanes])
            d_score = (prob * (d_prob - delta_ref[qs, :, lanes])).astype(jnp.bfloat16)
            probs.append((prob.astype(jnp.bfloat16), d_score))
        for (query, grad, keys, _, _), (prob, d_score) in zip(scores, probs):
            grads.append((dot(prob, grad, NN), dot(d_score, query, NN), dot(d_score, keys, TN)))
        for (ks, bs, qs, lanes, n), (d_value, d_key, d_query) in zip(work, grads):
            before = [(dk_acc[rows_of(a), lanes], dv_acc[rows_of(a), lanes]) for a in bs]
            for j, a in enumerate(bs):
                part = slice(j * BLOCK, (j + 1) * BLOCK)
                dk_acc[rows_of(a), lanes] = before[j][0] + d_key[part]
                dv_acc[rows_of(a), lanes] = before[j][1] + d_value[part]
            d_query = fold_heads(d_query, diags[n], n) * scale
            dq_ref[rows_of(qs), lanes] = d_query.astype(jnp.bfloat16)
        return carry

    lax.fori_loop(0, (nb - 2) // abreast, several, 0)
    dk_ref[...] = dk_acc[: nb * BLOCK].astype(jnp.bfloat16)
    dv_ref[...] = dv_acc[: nb * BLOCK].astype(jnp.bfloat16)


VMEM = pl.BlockSpec(memory_space=pltpu.VMEM)
SMEM = pl.BlockSpec(memory_space=pltpu.SMEM)


def columns(array, at, width):
    if array.shape[1] == width or width % 128 == 0:
        return array, pl.BlockSpec((array.shape[0], width), lambda i: (0, at))
    array = array[:, at * width : (at + 1) * width]
    return array, pl.BlockSpec(array.shape, lambda i: (0, 0))


def attend(qkv, tables, heads, nb):
    key_at, _, query_at, _, task_bias, lead_bias = tables
    width = heads * HEAD
    operands, specs = zip(*[columns(qkv, i, width) for i in range(3)])
    return pl.pallas_call(
        partial(attend_kernel, heads, nb, 2),
        grid=(1,),
        out_shape=(
            jax.ShapeDtypeStruct((nb * BLOCK, width), jnp.bfloat16),
            jax.ShapeDtypeStruct((nb, 1, width), jnp.float32),
        ),
        in_specs=[SMEM] * 2 + list(specs) + [VMEM] * 2,
        out_specs=(VMEM, VMEM),
        compiler_params=pltpu.CompilerParams(vmem_limit_bytes=48 << 20),
        cost_estimate=pl.CostEstimate(
            flops=20_000_000_000, bytes_accessed=8 << 20, transcendentals=0
        ),
        name="attend",
    )(key_at, query_at, *operands, task_bias, lead_bias)


def attend_back(qkv, grads, context, lse, tables, heads, nb, held, at):
    key_at, bias_at, query_at, bias, _, _ = tables
    total = context.shape[1]
    width = heads * HEAD
    parts = total // width
    operands, specs = zip(
        *[columns(qkv, i * parts + at, width) for i in range(3)], columns(context, at, width)
    )
    pieces, piece_specs = zip(*[columns(g, at, width) for g in grads])
    lse_spec = pl.BlockSpec((nb, 1, width), lambda i: (0, 0, at))
    out = jax.ShapeDtypeStruct((nb * BLOCK, total), jnp.bfloat16)
    out_spec = pl.BlockSpec((nb * BLOCK, width), lambda i: (0, at))
    count = 3 + len(operands) + 2 + len(pieces)
    abreast = 5 if (nb - 2) % 5 == 0 else 2
    return pl.pallas_call(
        partial(attend_back_kernel, heads, nb, abreast, len(pieces)),
        grid=(1,),
        out_shape=(out, out, out),
        in_specs=[SMEM] * 3
        + list(specs)
        + [lse_spec, VMEM]
        + list(piece_specs)
        + [pl.BlockSpec(memory_space=pl.ANY)] * len(held),
        out_specs=(out_spec,) * 3,
        input_output_aliases={count + i: i for i in range(len(held))},
        scratch_shapes=[
            pltpu.VMEM(((nb + 1) * BLOCK, width), jnp.float32),
            pltpu.VMEM(((nb + 1) * BLOCK, width), jnp.float32),
            pltpu.VMEM((nb, 1, width), jnp.float32),
            pltpu.VMEM((nb * BLOCK, width), jnp.bfloat16),
        ],
        compiler_params=pltpu.CompilerParams(vmem_limit_bytes=52 << 20),
        cost_estimate=pl.CostEstimate(
            flops=15_000_000_000, bytes_accessed=6 << 20, transcendentals=0
        ),
        name="attend_back",
    )(key_at, bias_at, query_at, *operands, lse, bias, *pieces, *held)


def block_tables(block_of_slot, doc, random_blocks):
    nb = random_blocks.shape[0]
    every = jnp.arange(nb, dtype=jnp.int32)
    slot_of_block = jnp.sum(
        jnp.where(block_of_slot[None, :] == every[:, None], every[None, :], 0), 1
    )
    ids = every[2:]
    before, after = ids - 1, ids + 1
    always_on = ids >= 0
    index = jnp.concatenate(
        [jnp.stack([ids * 0, ids * 0 + 1, before, ids, after], -1), random_blocks[2:]], -1
    )
    allowed = jnp.stack(
        [always_on, always_on, before >= 2, always_on, after < nb] + [always_on] * 3, -1
    )
    index = jnp.clip(index, 0, nb - 1)
    slots = jnp.sum(jnp.where(index[..., None] == block_of_slot, every, 0), -1)
    key_at = slots
    bias_at = jnp.where(allowed, slots, nb)
    query_at = jnp.concatenate([slot_of_block[2:], slot_of_block[:2]])
    inside = jnp.arange(BLOCK, dtype=jnp.int32)
    bias = jnp.where(block_of_slot[:, None] * BLOCK + inside < doc, 0.0, NEG_FILL)
    bias = bias.astype(jnp.float32)
    lead_bias = bias.reshape(1, -1)
    task_bias = (index[..., None] * BLOCK + inside < doc) & allowed[..., None]
    task_bias = jnp.where(task_bias, 0.0, NEG_FILL).astype(jnp.float32).reshape(nb - 2, -1)
    bias = jnp.concatenate([bias.reshape(-1), jnp.full((BLOCK,), NEG_FILL, jnp.float32)])
    bias = jnp.broadcast_to(bias[:, None], (bias.shape[0], 2 * HEAD))
    return key_at, bias_at, query_at, bias, task_bias, lead_bias


TANH_SCALE = 0.7978845608028654
TANH_CUBE = 0.044715


def norm_rows(value):
    center = value - jnp.mean(value, -1, keepdims=True)
    scale = lax.rsqrt(jnp.mean(center * center, -1, keepdims=True) + EPSILON)
    return center * scale, scale


def norm_back(grad, normal, scale):
    return scale * (
        grad
        - jnp.mean(grad, -1, keepdims=True)
        - normal * jnp.mean(grad * normal, -1, keepdims=True)
    )


def feed_forward_kernel(
    chunk,
    few,
    pieces,
    mine_ref,
    x_ref,
    cot_own_ref,
    cot_came_ref,
    wo_ref,
    w1_hbm_ref,
    w2_hbm_ref,
    vec_ref,
    b1_ref,
    *refs,
):
    context_refs, refs = refs[:pieces], refs[pieces:]
    result_ref, first_ref, active_out_ref, d_inner_out_ref, d_outer_ref, d_attended_ref = refs[:6]
    d_resid_ref, sums_ref, inner_sum_ref = refs[6:9]
    d_context_refs, refs = refs[9 : 9 + pieces], refs[9 + pieces :]
    w1_ref, w2_ref, active_ref, d_inner_ref, *refs = refs
    slope_ref, held_ref, normal_ref, scale_ref, acc_ref, sems = refs
    cols = D // pieces
    first_step = pl.program_id(0) == 0
    tile = active_ref.shape[0]
    tokens_at = pl.ds(pl.multiple_of(pl.program_id(0) * tile, tile), tile)
    load_w1 = pltpu.make_async_copy(w1_hbm_ref, w1_ref, sems.at[0])
    load_w2 = pltpu.make_async_copy(w2_hbm_ref, w2_ref, sems.at[1])
    store_active = pltpu.make_async_copy(active_ref, active_out_ref.at[tokens_at, :], sems.at[2])
    store_d_inner = pltpu.make_async_copy(d_inner_ref, d_inner_out_ref.at[tokens_at, :], sems.at[3])
    low, full = jnp.bfloat16, jnp.float32
    tokens, hidden = active_ref.shape

    @pl.when(first_step)
    def _():
        load_w1.start()
        load_w2.start()
        sums_ref[...] = jnp.zeros_like(sums_ref)
        inner_sum_ref[...] = jnp.zeros_like(inner_sum_ref)

    bo, g1, s1, b2, g2, s2 = [vec_ref[i : i + 1, :] for i in range(6)]

    def each_rows(body):
        def step(i, carry):
            body(pl.ds(pl.multiple_of(i * few, few), few))
            return carry

        lax.fori_loop(0, tokens // few, step, 0)

    def each_columns(body):
        def step(i, carry):
            body(pl.ds(pl.multiple_of(i * chunk, chunk), chunk))
            return carry

        lax.fori_loop(0, hidden // chunk, step, 0)

    def add_sum(row, values):
        sums_ref[row : row + 1, :] += jnp.sum(values, 0, keepdims=True)

    for k, ref in enumerate(context_refs):
        part = dot(ref[...], wo_ref[k * cols : (k + 1) * cols, :], NN)
        acc_ref[...] = part if k == 0 else acc_ref[...] + part

    @each_rows
    def _(rows):
        normal, scale = norm_rows(x_ref[rows, :].astype(full) + acc_ref[rows, :] + bo)
        first = normal * g1 + s1
        normal_ref[rows, :] = normal
        scale_ref[rows, :] = jnp.broadcast_to(scale, (few, 128))
        held_ref[rows, :] = first
        first_ref[rows, :] = first.astype(low)

    @pl.when(first_step)
    def _():
        load_w1.wait()

    @each_columns
    def _(cols):
        u = dot(first_ref[...], w1_ref[:, cols], NN) + b1_ref[:1, cols]
        square = u * u
        tanh = jnp.tanh(u * (TANH_SCALE + (TANH_SCALE * TANH_CUBE) * square))
        share = 0.5 * tanh + 0.5
        active_ref[:, cols] = (u * share).astype(low)
        slope_ref[:, cols] = share + (0.5 * u) * (1.0 - tanh * tanh) * (
            TANH_SCALE + (3 * TANH_SCALE * TANH_CUBE) * square
        )

    store_active.start()

    @pl.when(first_step)
    def _():
        load_w2.wait()

    acc_ref[...] = dot(active_ref[...], w2_ref[...], NN)

    @each_rows
    def _(rows):
        normal, scale = norm_rows(held_ref[rows, :] + acc_ref[rows, :] + b2)
        result_ref[rows, :] = (normal * g2 + s2).astype(low)
        own = pl.program_id(0) == 0
        cot = jnp.where(own, cot_own_ref[0, rows, :], cot_came_ref[rows, :]).astype(full)
        d_second = norm_back(cot * g2, normal, scale)
        held_ref[rows, :] = d_second
        d_outer = d_second.astype(low)
        d_outer_ref[rows, :] = d_outer
        add_sum(3, d_outer.astype(full))
        add_sum(4, cot * normal)
        add_sum(5, cot)

    @each_columns
    def _(cols):
        d_inner = (dot(d_outer_ref[...], w2_ref[cols, :], NT) * slope_ref[:, cols]).astype(low)
        d_inner_ref[:, cols] = d_inner
        inner_sum_ref[:1, cols] += jnp.sum(d_inner.astype(full), 0, keepdims=True)

    store_d_inner.start()
    acc_ref[...] = dot(d_inner_ref[...], w1_ref[...], NT)

    @each_rows
    def _(rows):
        d_first = held_ref[rows, :] + acc_ref[rows, :]
        normal = normal_ref[rows, :]
        add_sum(1, d_first * normal)
        add_sum(2, d_first)
        d_resid = norm_back(d_first * g1, normal, scale_ref[rows, :1])
        d_resid_ref[rows, :] = d_resid
        d_attended = d_resid.astype(low)
        d_attended_ref[rows, :] = d_attended
        add_sum(0, d_attended.astype(full))

    for k, ref in enumerate(d_context_refs):
        ref[...] = dot(d_attended_ref[...], wo_ref[k * cols : (k + 1) * cols, :], NT).astype(low)
    store_active.wait()
    store_d_inner.wait()


def feed_forward(mine, x, cot, cot_came, context, wo, w1, w2, vec, b1):
    low, full = jnp.bfloat16, jnp.float32
    tile, hidden = cot_came.shape[0], w1.shape[1]
    tokens, cols = 2 * tile, context[0].shape[1]
    row = pl.BlockSpec((tile, D), lambda i, at: (i, 0))
    part = pl.BlockSpec((tile, cols), lambda i, at: (i, 0))
    there = pl.BlockSpec(memory_space=pl.ANY)
    once = pl.Buffered(1)
    whole = lambda a: pl.BlockSpec(a.shape, lambda i, at: (0,) * a.ndim, pipeline_mode=once)
    shape = jax.ShapeDtypeStruct
    return pl.pallas_call(
        partial(feed_forward_kernel, 1024, 256, len(context)),
        grid_spec=pltpu.PrefetchScalarGridSpec(
            num_scalar_prefetch=1,
            grid=(tokens // tile,),
            in_specs=[
                row,
                pl.BlockSpec((1, tile, D), lambda i, at: (at[0], 0, 0), pipeline_mode=once),
            ]
            + [whole(cot_came), whole(wo), there, there, whole(vec), whole(b1)]
            + [part] * len(context),
            out_specs=[row, row, there, there, row, row, row]
            + [pl.BlockSpec((8, n), lambda i, at: (0, 0)) for n in (D, hidden)]
            + [part] * len(context),
            scratch_shapes=[
                pltpu.VMEM(w1.shape, low),
                pltpu.VMEM(w2.shape, low),
                pltpu.VMEM((tile, hidden), low),
                pltpu.VMEM((tile, hidden), low),
                pltpu.VMEM((tile, hidden), full),
                pltpu.VMEM((tile, D), full),
                pltpu.VMEM((tile, D), full),
                pltpu.VMEM((tile, 128), full),
                pltpu.VMEM((tile, D), full),
                pltpu.SemaphoreType.DMA((4,)),
            ],
        ),
        out_shape=[
            shape((tokens, D), low),
            shape((tokens, D), low),
            shape((tokens, hidden), low),
            shape((tokens, hidden), low),
            shape((tokens, D), low),
            shape((tokens, D), low),
            shape((tokens, D), full),
            shape((8, D), full),
            shape((8, hidden), full),
        ]
        + [shape((tokens, cols), low)] * len(context),
        compiler_params=pltpu.CompilerParams(vmem_limit_bytes=58 << 20),
        cost_estimate=pl.CostEstimate(
            flops=50_000_000_000, bytes_accessed=40 << 20, transcendentals=0
        ),
        name="feed_forward",
    )(jnp.reshape(mine, (1,)).astype(jnp.int32), x, cot, cot_came, wo, w1, w2, vec, b1, *context)


def wide_kernel(at_ref, left_ref, right_ref, *refs):
    *came_refs, out_ref, turned_ref = refs
    i = pl.program_id(0)

    @pl.when(i == 0)
    def _():
        turned_ref[...] = left_ref[...].T

    rows = out_ref.shape[0]
    some = pl.ds(pl.multiple_of(lax.rem(i, D // rows) * rows, rows), rows)
    out_ref[...] = add_came(dot(turned_ref[some, :], right_ref[...], NN), came_refs)


def add_came(total, came_refs):
    for ref in came_refs:
        total = total + ref[...].astype(jnp.float32)
    return total.astype(jnp.bfloat16)


def tall_kernel(at_ref, left_ref, right_ref, *refs):
    *came_refs, out_ref = refs
    out_ref[...] = add_came(dot(left_ref[...], right_ref[...], TN), came_refs)


def tall_product(left, right, half, count, tile, came=()):
    tokens, width = right.shape[0], left.shape[1]
    part = width // count
    per = part // tile
    return pl.pallas_call(
        tall_kernel,
        grid_spec=pltpu.PrefetchScalarGridSpec(
            num_scalar_prefetch=1,
            grid=(per,),
            in_specs=[
                pl.BlockSpec((tokens, tile), lambda i, at: (0, at[0] * per + i)),
                pl.BlockSpec((tokens, right.shape[1]), lambda i, at: (0, 0)),
            ]
            + [pl.BlockSpec((tile, right.shape[1]), lambda i, at: (i, 0))] * len(came),
            out_specs=pl.BlockSpec((tile, right.shape[1]), lambda i, at: (i, 0)),
        ),
        out_shape=jax.ShapeDtypeStruct((part, right.shape[1]), jnp.bfloat16),
        compiler_params=pltpu.CompilerParams(vmem_limit_bytes=48 << 20),
        cost_estimate=pl.CostEstimate(
            flops=2 * tokens * part * right.shape[1], bytes_accessed=8 << 20, transcendentals=0
        ),
        name="tall_product",
    )(jnp.reshape(half, (1,)).astype(jnp.int32), left, right, *came)


def wide_product(left, right, half, count, rows, came=()):
    tokens, width = right.shape
    part = width // count
    blocks, per = part // D, D // rows
    return pl.pallas_call(
        wide_kernel,
        grid_spec=pltpu.PrefetchScalarGridSpec(
            num_scalar_prefetch=1,
            grid=(blocks * per,),
            in_specs=[
                pl.BlockSpec((tokens, D), lambda i, at: (0, 0)),
                pl.BlockSpec((tokens, D), lambda i, at: (0, at[0] * blocks + i // per)),
            ]
            + [pl.BlockSpec((rows, D), lambda i, at: (i, 0))] * len(came),
            out_specs=pl.BlockSpec((rows, D), lambda i, at: (i, 0)),
            scratch_shapes=[pltpu.VMEM((D, tokens), jnp.bfloat16)],
        ),
        out_shape=jax.ShapeDtypeStruct((part, D), jnp.bfloat16),
        compiler_params=pltpu.CompilerParams(vmem_limit_bytes=48 << 20),
        cost_estimate=pl.CostEstimate(
            flops=2 * tokens * part * D, bytes_accessed=8 << 20, transcendentals=0
        ),
        name="wide_product",
    )(jnp.reshape(half, (1,)).astype(jnp.int32), left, right, *came)


def heads_kernel(x_ref, d_query_ref, d_key_ref, d_value_ref, out_ref, turned_ref):
    tokens, rows = x_ref.shape[0], turned_ref.shape[0]

    @pl.when(pl.program_id(0) == 0)
    def _():
        turned_ref[:D, :] = x_ref[...].T
        row = lax.broadcasted_iota(jnp.int32, (rows - D, tokens), 0)
        turned_ref[D:, :] = (row == 0).astype(jnp.float32).astype(jnp.bfloat16)

    for i, ref in enumerate((d_query_ref, d_key_ref, d_value_ref)):

        @pl.when(pl.program_id(0) == i)
        def _():
            out_ref[...] = dot(turned_ref[...], ref[...], NN).astype(jnp.bfloat16)


def heads_products(x, d_query, d_key, d_value):
    tokens, cols = d_query.shape
    rows = D + 32
    each = pl.BlockSpec((tokens, cols), lambda i: (0, 0))
    return pl.pallas_call(
        heads_kernel,
        grid=(3,),
        in_specs=[pl.BlockSpec((tokens, D), lambda i: (0, 0)), each, each, each],
        out_specs=pl.BlockSpec((rows, cols), lambda i: (0, i)),
        out_shape=jax.ShapeDtypeStruct((rows, 3 * cols), jnp.bfloat16),
        scratch_shapes=[pltpu.VMEM((rows, tokens), jnp.bfloat16)],
        compiler_params=pltpu.CompilerParams(vmem_limit_bytes=48 << 20),
        cost_estimate=pl.CostEstimate(
            flops=6 * tokens * rows * cols, bytes_accessed=8 << 20, transcendentals=0
        ),
        name="heads_products",
    )(x, d_query, d_key, d_value)


def spread_heads_kernel(at_ref, pool_ref, *refs):
    for i, ref in enumerate(refs[-3:]):

        @pl.when(pl.program_id(0) == i)
        def _():
            ref[...] = pool_ref[...].astype(jnp.float32)


def spread_columns(pool, half, held):
    cols = pool.shape[1] // 3
    shape = jax.ShapeDtypeStruct((D, D), jnp.float32)
    return pl.pallas_call(
        spread_heads_kernel,
        grid_spec=pltpu.PrefetchScalarGridSpec(
            num_scalar_prefetch=1,
            grid=(3,),
            in_specs=[pl.BlockSpec((D, cols), lambda i, at: (0, i))]
            + [pl.BlockSpec(memory_space=pl.ANY)] * len(held),
            out_specs=[pl.BlockSpec((D, cols), lambda i, at: (0, at[0]))] * 3,
        ),
        out_shape=[shape] * 3,
        input_output_aliases={2 + i: i for i in range(len(held))},
        compiler_params=pltpu.CompilerParams(vmem_limit_bytes=32 << 20),
        cost_estimate=SHORT,
        name="spread_columns",
    )(jnp.reshape(half, (1,)).astype(jnp.int32), pool, *held)


def spread_outer_kernel(at_ref, first_ref, second_ref, *refs):
    i, blocks = pl.program_id(0), pl.num_programs(0)

    @pl.when(i < blocks - 1)
    def _():
        refs[-1][...] = first_ref[...].astype(jnp.float32)

    @pl.when(i == blocks - 1)
    def _():
        refs[-1][...] = second_ref[...].astype(jnp.float32)


def spread_inner_kernel(at_ref, first_ref, second_ref, third_ref, *refs):
    inner_ref, out_ref = refs[-2:]
    i, blocks = pl.program_id(0), pl.num_programs(0) - 1

    @pl.when(i < blocks - 1)
    def _():
        inner_ref[...] = first_ref[...].astype(jnp.float32)

    @pl.when(i == blocks - 1)
    def _():
        inner_ref[...] = second_ref[...].astype(jnp.float32)

    @pl.when(i == blocks)
    def _():
        out_ref[...] = third_ref[...].astype(jnp.float32)


def spread_call(kernel, name, half, grid, operands, specs, out_shapes, out_specs, held):
    return pl.pallas_call(
        kernel,
        grid_spec=pltpu.PrefetchScalarGridSpec(
            num_scalar_prefetch=1,
            grid=grid,
            in_specs=specs + [pl.BlockSpec(memory_space=pl.ANY)] * len(held),
            out_specs=out_specs,
        ),
        out_shape=[jax.ShapeDtypeStruct(s, jnp.float32) for s in out_shapes],
        input_output_aliases={1 + len(operands) + i: i for i in range(len(held))},
        compiler_params=pltpu.CompilerParams(vmem_limit_bytes=32 << 20),
        cost_estimate=SHORT,
        name=name,
    )(jnp.reshape(half, (1,)).astype(jnp.int32), *operands, *held)


def spread_outer(first, second, half, held):
    rows = second.shape[0]
    blocks = first.shape[0] // rows + 1
    return spread_call(
        spread_outer_kernel,
        "spread_outer",
        half,
        (blocks,),
        (first, second),
        [
            pl.BlockSpec((rows, D), lambda i, at: (jnp.minimum(i, blocks - 2), 0)),
            pl.BlockSpec((rows, D), lambda i, at: (0, 0)),
        ],
        [(2 * rows * blocks, D)],
        [pl.BlockSpec((rows, D), lambda i, at: (at[0] * blocks + i, 0))],
        held,
    )


def spread_inner(first, mixed, half, held):
    rows = 256
    per = D // rows
    blocks = first.shape[0] // rows + 1
    wide = blocks // per
    out_rows = D // 2

    def inner_at(i, at):
        j = jnp.minimum(i, blocks - 1)
        return (j % per, at[0] * wide + j // per)

    return spread_call(
        spread_inner_kernel,
        "spread_inner",
        half,
        (blocks + 1,),
        (first, mixed, mixed),
        [
            pl.BlockSpec((rows, D), lambda i, at: (jnp.minimum(i, blocks - 2), 0)),
            pl.BlockSpec((rows, D), lambda i, at: (mixed.shape[0] // rows - 1, 0)),
            pl.BlockSpec((out_rows, D), lambda i, at: (0, 0)),
        ],
        [(D, 2 * wide * D), (D, D)],
        [
            pl.BlockSpec((rows, D), inner_at),
            pl.BlockSpec((out_rows, D), lambda i, at: (at[0], 0)),
        ],
        held,
    )


class Ring:
    def __init__(self, axis, size, at, perm):
        self.axis, self.size, self.at, self.perm = axis, size, at, perm

    def send(self, value, by):
        return lax.ppermute(value, self.axis, self.perm(by))


class Pairs:
    def __init__(self, seq, rows, masks, core):
        me = lax.axis_index("seq") * rows + lax.axis_index("rows")
        bits = [lax.rem(me // mask, 2) for mask in masks]
        self.bit = jnp.where(lax.rem(me // core, 2) == 0, bits[0], bits[1])
        self.perm = [(i, i ^ masks[i // core % 2]) for i in range(seq * rows)]

    def swap(self, value):
        return lax.ppermute(value, ("seq", "rows"), self.perm)

    def keep(self, value):
        part = value.shape[0] // 2
        return lax.dynamic_slice_in_dim(value, self.bit * part, part, 0)

    def give(self, value):
        part = value.shape[0] // 2
        return lax.dynamic_slice_in_dim(value, (1 - self.bit) * part, part, 0)

    def halved(self, value, came):
        return (self.keep(value).astype(jnp.float32) + came.astype(jnp.float32)).astype(value.dtype)

    def halve(self, value):
        return self.halved(value, self.swap(self.give(value)))

    def joined(self, value, came):
        first = jnp.where(self.bit == 0, value, came)
        second = jnp.where(self.bit == 0, came, value)
        return jnp.concatenate([first, second], 0)

    def join(self, value):
        return self.joined(value, self.swap(value))


def powers(step, count):
    masks = []
    while count > 1:
        masks.append(step)
        step, count = step * 2, count // 2
    return masks


def make_links(seq, rows):
    half = seq // 2
    deep = CHIPS_Z if rows % CHIPS_Z == 0 else 1
    wide = rows // deep
    s = lax.axis_index("seq")
    near = Ring(
        "seq",
        half,
        lax.rem(s, half),
        lambda by: [(i, i // half * half + (i + by) % half) for i in range(seq)],
    )

    def pairs(first, second=None):
        return Pairs(seq, rows, (first, second or first), rows)

    far_mask = half * rows
    y, z = powers(1, wide), powers(wide, deep)
    far = pairs(far_mask)
    inside = [pairs(mask) for mask in powers(rows, half)]
    main = [pairs(far_mask, y[0]), pairs(y[0], z[0]), pairs(z[0], far_mask)]
    side = [pairs(z[0]), pairs(far_mask), pairs(y[0])]
    last = [pairs(mask) for mask in y[1:] + z[1:]]
    return near, far, inside, [main, side], last


def in_step(values):
    return list(lax.optimization_barrier(tuple(values)))


def cut(value, sizes):
    out, at = [], 0
    for size in sizes:
        out.append(value[at : at + size])
        at += size
    return out


class HalveStep:
    def __init__(self, pairs):
        self.pairs = pairs

    def start(self, parts):
        return [pair.swap(pair.give(part)) for pair, part in zip(self.pairs, parts)]

    def finish(self, parts, came):
        return [pair.halved(*both) for pair, *both in zip(self.pairs, parts, came)]


class JoinStep:
    def __init__(self, pairs):
        self.pairs = pairs

    def start(self, parts):
        return [pair.swap(part) for pair, part in zip(self.pairs, parts)]

    def finish(self, parts, came):
        return [pair.joined(*both) for pair, *both in zip(self.pairs, parts, came)]


class SumStep:
    def __init__(self, pair):
        self.pair = pair

    def start(self, parts):
        return cut(self.pair.swap(jnp.concatenate(parts, 0)), [p.shape[0] for p in parts])

    def finish(self, parts, came):
        return [
            (p.astype(jnp.float32) + c.astype(jnp.float32)).astype(p.dtype)
            for p, c in zip(parts, came)
        ]


class Chain:
    def __init__(self, parts, steps):
        self.parts, self.steps, self.came = list(parts), list(steps), None

    def start(self):
        self.came = self.steps[0].start(self.parts)

    def finish(self, *after):
        came = in_step(list(self.came) + list(after))[: len(self.came)]
        self.parts = self.steps.pop(0).finish(self.parts, came)
        self.came = None

    def step(self, *after):
        if self.came is None:
            self.start()
        self.finish(*after)
        if self.steps:
            self.start()


def column_sum(values):
    return jnp.sum(values.astype(jnp.float32), 0)


def per_device(
    seq,
    rows,
    inputs,
    query_weight,
    query_bias,
    key_weight,
    value_weight,
    value_bias,
    output_weight,
    output_bias,
    first_gain,
    first_shift,
    inner_weight,
    inner_bias,
    outer_weight,
    outer_bias,
    second_gain,
    second_shift,
    doc_tokens,
    random_blocks,
    cotangent,
):
    low, full = jnp.bfloat16, jnp.float32
    near, far, inside, routes, last = make_links(seq, rows)
    main, side = routes
    half = seq // 2
    width = inputs.shape[1]
    tokens = 2 * width
    nb = random_blocks.shape[1]
    heads = HEADS // half
    cols = heads * HEAD
    mine, at = far.bit, near.at

    def own_and_other(array):
        own = lax.dynamic_index_in_dim(array, mine, 0, False)
        return own, lax.dynamic_index_in_dim(array, 1 - mine, 0, False)

    def from_rows(own, other):
        return jnp.where(mine == 0, jnp.stack([own, other]), jnp.stack([other, own]))

    def by_device(values):
        stacked = jnp.stack(values)
        order = lax.rem(at + half - jnp.arange(half), half)
        return jnp.take(stacked, order, axis=0) if half > 2 else jnp.where(at == 0, stacked, stacked[::-1])

    def by_two(values):
        return [values[i : i + 2] for i in range(0, len(values), 2)]

    x_own, x_other = own_and_other(inputs)
    x_came = far.swap(x_other)

    shards = []
    for k in range(half):
        own = mine * half + lax.rem(at + k, half)
        shards += [own, lax.rem(own + half, seq)]
    per_shard = width // BLOCK
    block_of_slot = (
        jnp.stack(shards)[:, None] * per_shard + jnp.arange(per_shard, dtype=jnp.int32)
    ).reshape(-1).astype(jnp.int32)
    doc = lax.dynamic_index_in_dim(doc_tokens, mine, 0, False)
    chosen = lax.dynamic_index_in_dim(random_blocks, mine, 0, False)
    tables = block_tables(block_of_slot, doc, chosen)

    def my_cols(weight):
        return lax.dynamic_slice_in_dim(weight, at * cols, cols, weight.ndim - 1)

    w_qkv = jnp.concatenate([my_cols(w) for w in (query_weight, key_weight, value_weight)], 1)
    b_qkv = jnp.concatenate(
        [my_cols(query_bias), jnp.zeros((cols,), low), my_cols(value_bias)]
    ).astype(full)
    wo = jnp.concatenate(
        [
            lax.dynamic_slice_in_dim(
                output_weight, lax.rem(at + half - k, half) * cols, cols, 0
            )
            for k in range(half)
        ],
        0,
    )
    vec = jnp.stack(
        [output_bias, first_gain, first_shift, outer_bias, second_gain, second_shift]
    ).astype(full)
    vec = jnp.pad(vec, ((0, 2), (0, 0)))
    b1 = jnp.broadcast_to(inner_bias.astype(full), (8, inner_bias.shape[0]))

    x_came, w_qkv, b_qkv, wo, vec, b1, *tables = in_step(
        [x_came, w_qkv, b_qkv, wo, vec, b1, *tables]
    )
    x_parts = [x_own, x_came]
    for k in range(1, half):
        x_parts += [near.send(x_own, half - k), near.send(x_came, half - k)]
    x_all, cotangent = in_step([jnp.concatenate(x_parts, 0), cotangent])
    cot_came = far.swap(lax.dynamic_index_in_dim(cotangent, 1 - mine, 0, False))
    qkv = (dot(x_all, w_qkv, NN) + b_qkv).astype(low)
    qkv, cotangent = in_step([qkv, cotangent])
    heads_context, lse = attend(qkv, tables, heads, nb)
    heads_context, lse, cot_came = in_step([heads_context, lse, cot_came])
    context = [heads_context] + [
        near.send(heads_context[k * tokens : (k + 1) * tokens], k) for k in range(1, half)
    ]
    (
        result,
        first_low,
        active,
        d_inner,
        d_outer,
        d_attended,
        d_resid,
        sums,
        inner_sum,
        *d_context,
    ) = feed_forward(
        mine, x_all, cotangent, cot_came, context, wo, inner_weight, outer_weight, vec, b1
    )
    heads_grad = [d_context[0]] + [near.send(d_context[k], half - k) for k in range(1, half)]

    packed = jnp.concatenate([sums[:6].reshape(-1), inner_sum[0]]).reshape(-1, D)
    packed = jnp.pad(packed, ((0, 256 - packed.shape[0]), (0, 0))).astype(low)

    def outer_product(part, k, came=()):
        return tall_product(active, d_outer, part, half, 768, came)

    def inner_product(part, k, came=()):
        return wide_product(first_low, d_inner, part, half, 768, came)

    def out_product(part, k, came=()):
        k = (half - k) % half
        if cols % 128:
            total = dot(context[k][:tokens], d_attended, TN)
            return sum([c.astype(full) for c in came], total).astype(low)
        return tall_product(context[k], d_attended, 0, 1, cols, came)

    def packed_part(part, k, came=()):
        size = 256 // half
        total = lax.dynamic_slice_in_dim(packed, part * size, size, 0).astype(full)
        return sum([c.astype(full) for c in came], total).astype(low)

    def give(product):
        return [product(lax.rem(at + k, half), k) for k in range(1, half)]

    def send(parts):
        return [near.send(part, k) for k, part in enumerate(parts, 1)]

    outer_give = give(outer_product)
    outer_give[0], first_low, d_attended = in_step([outer_give[0], first_low, d_attended])
    outer_came = send(outer_give)
    inner_came = send(give(inner_product))
    out_came = send(give(out_product))
    packed_came = send(give(packed_part))
    outer_grad = outer_product(at, 0, outer_came)
    outer_main = outer_grad.shape[0] * 3 // 4
    early = Chain([outer_grad[:outer_main], outer_grad[outer_main:]], [HalveStep([main[0], side[0]])])
    early.start()
    inner_came[0], out_came[0], packed_came[0], *early.parts = in_step(
        [inner_came[0], out_came[0], packed_came[0]] + early.parts
    )
    inner_grad = inner_product(at, 0, inner_came)
    out_grad = out_product(at, 0, out_came)
    packed = packed_part(at, 0, packed_came)
    inner_grad, out_grad, packed, *early.came = in_step(
        [inner_grad, out_grad, packed] + early.came
    )
    early.finish()
    inner_main = inner_grad.shape[0] * 5 // 6
    mixed = jnp.concatenate([out_grad, packed, inner_grad[inner_main:]], 0)
    rest = Chain([inner_grad[:inner_main], mixed], [HalveStep([main[0], side[0]])])
    heads_grad[0], *rest.parts = in_step([heads_grad[0]] + early.parts + rest.parts)
    early.parts, rest.parts = rest.parts[:2], rest.parts[2:]

    first_sizes = [
        (outer_main // 2, inner_main // 2),
        ((outer_grad.shape[0] - outer_main) // 2, mixed.shape[0] // 2),
    ]
    first = Chain([], [HalveStep([main[i], side[i]]) for i in (1, 2)])
    first.steps += [SumStep(pair) for pair in last]
    first.steps += [JoinStep([main[i], side[i]]) for i in (2, 1)]

    steps = cols // 128 if cols % 128 == 0 else 1
    d_qkv = ()
    result_half = [result[width : width + width // 2], result[width + width // 2 :]]
    result_came = []
    for k in range(steps):
        chain = first if first.parts else rest
        chain.start()
        if k == 2:
            result_half[0], d_query = in_step([result_half[0], d_qkv[0]])
            d_qkv = (d_query,) + d_qkv[1:]
            result_came.append(far.swap(result_half[0]))
        d_qkv = attend_back(
            qkv, heads_grad, heads_context, lse, tables, heads // steps, nb, d_qkv, k
        )
        d_query, d_key, d_value, *came = in_step(list(d_qkv) + chain.came + result_came)
        d_qkv = (d_query, d_key, d_value)
        chain.came, result_came = came[: len(chain.came)], came[len(chain.came) :]
        chain.finish()
        if chain is rest:
            first.parts = [
                jnp.concatenate([e, r], 0) for e, r in zip(early.parts, rest.parts)
            ]
        d_query, *first.parts = in_step([d_query] + first.parts)
        d_qkv = (d_query, d_key, d_value)

    while len(first.steps) > 3:
        first.start()
        first.finish()
    sums_at_last = first.steps.pop(0)
    last_came = sums_at_last.start(first.parts[:1]) + sums_at_last.start(first.parts[1:])
    result_half[1:], d_query = in_step([*result_half[1:], d_query])[:-1], d_query
    result_came += [far.swap(piece) for piece in result_half[len(result_came) :]]
    if cols % 128 == 0:
        heads_part = heads_products(x_all, *d_qkv)
    else:
        sums_of = [jnp.pad(column_sum(d)[None, :], ((0, 31), (0, 0))) for d in d_qkv]
        heads_part = [
            jnp.concatenate([dot(x_all, d, TN), total], 0) for d, total in zip(d_qkv, sums_of)
        ]
        heads_part = jnp.concatenate(heads_part, 1).astype(low)
    heads_part, d_query, *result_came = in_step([heads_part, d_query] + result_came)

    second = Chain([heads_part], [HalveStep([main[i]]) for i in range(3)])
    second.steps += [SumStep(pair) for pair in last]
    second.steps += [JoinStep([main[i]]) for i in (2, 1, 0)]
    second.start()
    wq, wk, wv = (w_qkv[:, i * cols : (i + 1) * cols] for i in range(3))
    d_part = (dot(d_query, wq, NT) + dot(d_key, wk, NT) + dot(d_value, wv, NT)).astype(low)
    result = from_rows(result[:width], jnp.concatenate(result_came, 0))
    d_part, result, *came = in_step([d_part, result] + last_came + second.came)
    first.parts, second.came = sums_at_last.finish(first.parts, came[:2]), came[2:]
    second.finish()

    def together(*beside):
        count = len(first.came or ())
        values = in_step(list(first.came or ()) + second.came + list(beside))
        if count:
            first.came = values[:count]
            first.finish()
        second.came = values[count : count + len(second.came)]
        second.finish()
        return values[len(values) - len(beside) :]

    second.start()
    first.start()
    d_came = [near.send(d_part[k * tokens : (k + 1) * tokens], k) for k in range(1, half)]
    d_came = together(*d_came)
    second.start()
    first.start()
    d_input = d_resid + d_part[:tokens].astype(full)
    for value in d_came:
        d_input = d_input + value.astype(full)
    d_input = d_input.astype(low)
    (d_input,) = together(d_input)
    for _ in last[:-1]:
        second.step()
    second.start()
    pieces = [p for share, size in zip(first.parts, first_sizes) for p in cut(share, size)]
    outer = Chain([pieces[0], pieces[2]], [JoinStep([main[0], side[0]])])
    inner = Chain([pieces[1], pieces[3]], [JoinStep([main[0], side[0]])])
    outer.start()
    d_input_came = [far.swap(d_input[width : width + width // 2])]
    outer.came, inner.parts, d_input_came = (
        lambda v: (v[:2], v[2:4], v[4:])
    )(together(*outer.came, *inner.parts, *d_input_came))
    outer.finish()
    second.start()
    inner.start()
    outer_came = [near.send(part, k) for k in range(1, half) for part in outer.parts]
    placed = spread_outer(*outer.parts, at, ()) if half == 2 else outer.parts
    count = 2 + len(outer_came)
    values = together(*inner.came, *outer_came, d_input, *placed)
    inner.came, outer_came, d_input = values[:2], values[2:count], values[count]
    outer.parts = values[count + 1 :]
    inner.finish()
    second.start()
    inner_came = [near.send(part, k) for k in range(1, half) for part in inner.parts]
    d_input_came.append(far.swap(d_input[width + width // 2 :]))
    if half == 2:
        outer.parts = list(spread_outer(*outer_came, 1 - at, outer.parts))
    count = len(inner_came)
    values = together(*inner_came, *d_input_came, *outer.parts)
    inner_came, d_input_came, outer.parts = (
        values[:count],
        values[count : count + 2],
        values[count + 2 :],
    )
    second.start()
    d_input = from_rows(d_input[:width], jnp.concatenate(d_input_came, 0))
    small = out_grad.shape[0], packed.shape[0], inner_grad.shape[0] - inner_main
    out_grad, packed, inner_b = cut(inner.parts[1], small)
    packed = [packed] + [cut(p, small)[1] for p in inner_came[1::2]]
    packed = by_device(packed).reshape(-1, D).astype(full)
    if half == 2:
        (outer_grad,) = outer.parts
        placed = spread_inner(*inner.parts, at, ())
        inner_grad, out_grad = spread_inner(*inner_came, 1 - at, placed)
    else:
        outer_grad = [jnp.concatenate(p, 0) for p in [outer.parts] + by_two(outer_came)]
        outer_grad = by_device(outer_grad).reshape(-1, D).astype(full)
        inner_grad = [jnp.concatenate([inner.parts[0], inner_b], 0)]
        out_grad = [out_grad]
        for first_part, other in by_two(inner_came):
            inner_grad.append(jnp.concatenate([first_part, cut(other, small)[2]], 0))
            out_grad.append(cut(other, small)[0])
        inner_grad = by_device(inner_grad).reshape(-1, D, D).astype(full)
        inner_grad = inner_grad.transpose(1, 0, 2).reshape(D, -1)
        out_grad = by_device(out_grad).reshape(-1, D).astype(full)
    d_input, inner_grad, out_grad, outer_grad, packed = together(
        d_input, inner_grad, out_grad, outer_grad, packed
    )
    heads_parts = second.parts[0]
    if half == 2:
        heads_came = near.send(heads_parts, 1)
        query_grad, key_grad, value_grad = spread_columns(
            heads_came, 1 - at, spread_columns(heads_parts, at, ())
        )
        biases = [p[D].astype(full) for p in (heads_parts, heads_came)]
        biases = jnp.where(at == 0, jnp.stack(biases), jnp.stack(biases[::-1]))
        query_bias_grad = biases[:, :cols].reshape(-1)
        value_bias_grad = biases[:, 2 * cols :].reshape(-1)
    else:
        heads_parts = by_device([heads_parts] + [near.send(heads_parts, k) for k in range(1, half)])
        query_grad, key_grad, value_grad = (
            jnp.concatenate([p[:, i * cols : (i + 1) * cols] for p in heads_parts], 1).astype(full)
            for i in range(3)
        )
        query_bias_grad, value_bias_grad = query_grad[D], value_grad[D]
        query_grad, key_grad, value_grad = query_grad[:D], key_grad[:D], value_grad[:D]
    return (
        result,
        d_input,
        query_grad,
        query_bias_grad,
        key_grad,
        value_grad,
        value_bias_grad,
        out_grad,
        packed[0],
        packed[1],
        packed[2],
        inner_grad,
        packed[6:10].reshape(-1),
        outer_grad,
        packed[3],
        packed[4],
        packed[5],
    )


def solution(mesh):
    tokens = P("rows", "seq", None)
    in_specs = (tokens,) + (P(),) * 15 + (P("rows"), P("rows", None, None), tokens)
    out_specs = (tokens, tokens) + (P(),) * 15
    return jax.shard_map(
        partial(per_device, mesh.shape["seq"], mesh.shape["rows"]),
        mesh=mesh,
        in_specs=in_specs,
        out_specs=out_specs,
        check_vma=False,
    )
```

profile of v0, /device:TPU:0, one launch (start us, length us, event | category | flops | bytes accessed | tf_op | source)
XLA Modules:
  0.0 354.2 jit_solution(14911727116440129970)
XLA Ops:
  0.8 2.5 dynamic-slice_bitcast_fusion.2
  3.3 2.9 collective-permute-start
  17.8 6.3 %collective-permute-done = bf16[512,768]{1,0:T(8,128)(2,1)} collective-permute-done((bf16[512,768]{1,0:T(8,128)(2,1)}, bf16[512,768]{1,0:T(8,128)(2,1)}, u32[]{:S(2)}, u32[]{:S(2)}) %collective-permute-start) | collective-permute-done | bytes 786464 | tf_op jit(solution)/shard_map/ppermute | solution.py:812
  26.1 2.5 collective-permute-done.2
  30.2 5.9 %add_convert_fusion.q_ref.k_ref.v_ref = bf16[2048,1152]{1,0:T(8,128)(2,1)} fusion(bf16[2048,768]{1,0:T(8,128)(2,1)S(1)} %pad_maximum_fusion.x_ref, bf16[768,1152]{1,0:T(8,128)(2,1)S(1)} %pad_maximum_fusion.4, f32[1152]{0:T(1024)S(1)} %maximum_convert_fusion), kind=kOutput, calls=%fused_computation | convolution fusion | flops 3628597248 | bytes 9638400 | tf_op jit(solution)/shard_map/dot_general | solution.py:29
  36.1 1.7 collective-permute-start.3
  37.8 16.2 %attend.1 = (bf16[2048,384]{1,0:T(8,128)(2,1)S(1)}, f32[32,1,384]{2,1,0:T(1,128)S(1)}) custom-call(s32[30,8]{1,0:T(8,128)S(1)} %select_reduce_fusion.key_at_ref, s32[32]{0:T(128)S(1)} %pad_add_fusion.query_at_ref, bf16[2048,1152]{1,0:T(8,128)(2,1)} %add_convert_fusion.q_ref.k_ref.v_ref, bf16[2048,1152]{1,0:T(8,128)(2,1)} %add_convert_fusion.q_ref.k_ref.v_ref, ...), custom_call_target="tpu_custom_call" | custom-call | flops 20000000000 | bytes 8388608 | tf_op jit(solution)/shard_map/attend/pallas_call | solution.py:265
  54.0 1.7 collective-permute-done.3.cot_came_ref
  55.8 2.3 collective-permute-done.4.refs_1_.left_ref
  59.0 48.3 %feed_forward.1 = (bf16[1024,768]{1,0:T(8,128)(2,1)}, bf16[1024,768]{1,0:T(8,128)(2,1)}, bf16[1024,3072]{1,0:T(8,128)(2,1)}, bf16[1024,3072]{1,0:T(8,128)(2,1)},...) custom-call(s32[1]{0:T(128)} %bitcast.14.mine_ref, ...), custom_call_target="tpu_custom_call" | custom-call | flops 49999998976 | bytes 41943040 | tf_op jit(solution)/shard_map/feed_forward/pallas_call | solution.py:515
  108.7 5.4 %tall_product.4 = bf16[1536,768]{1,0:T(8,128)(2,1)} custom-call(s32[1]{0:T(128)} %bitcast.15.at_ref, bf16[1024,3072]{1,0:T(8,128)(2,1)} %get-tuple-element.194.left_ref, bf16[1024,768]{1,0:T(8,128)(2,1)S(1)} %copy-done.3), custom_call_target="tpu_custom_call" | custom-call | flops 2415919104 | bytes 8388608 | tf_op jit(solution)/shard_map/tall_product/pallas_call | solution.py:590
  114.3 6.0 %wide_product.2 = bf16[1536,768]{1,0:T(8,128)(2,1)} custom-call(s32[1]{0:T(128)} %bitcast.15.at_ref, bf16[1024,768]{1,0:T(8,128)(2,1)S(1)} %copy-done.2, bf16[1024,3072]{1,0:T(8,128)(2,1)} %get-tuple-element.199.right_ref), custom_call_target="tpu_custom_call" | custom-call | flops 2415919104 | bytes 8388608 | tf_op jit(solution)/shard_map/wide_product/pallas_call | solution.py:615
  124.6 2.1 slice_bitcast_fusion.1
  126.6 4.7 %tall_product.6 = bf16[1536,768]{1,0:T(8,128)(2,1)S(1)} custom-call(s32[1]{0:T(128)} %bitcast.16.at_ref, bf16[1024,3072]{1,0:T(8,128)(2,1)} %get-tuple-element.194.left_ref, bf16[1024,768]{1,0:T(8,128)(2,1)S(1)} %copy-done.4, bf16[1536,768]{1,0:T(8,128)(2,1)} %collective-permute-done.8.refs_0_), custom_call_target="tpu_custom_call" | custom-call | flops 2415919104 | bytes 8388608 | tf_op jit(solution)/shard_map/tall_product/pallas_call | solution.py:590
  132.5 1.7 collective-permute-start.9
  136.9 5.1 %wide_product.3 = bf16[1536,768]{1,0:T(8,128)(2,1)S(1)} custom-call(s32[1]{0:T(128)} %bitcast.16.at_ref, bf16[1024,768]{1,0:T(8,128)(2,1)S(1)} %copy-done.2, bf16[1024,3072]{1,0:T(8,128)(2,1)} %get-tuple-element.199.right_ref, bf16[1536,768]{1,0:T(8,128)(2,1)} %collective-permute-done.5.refs_0_), custom_call_target="tpu_custom_call" | custom-call | flops 2415919104 | bytes 8388608 | tf_op jit(solution)/shard_map/wide_product/pallas_call | solution.py:615
  148.6 1.8 collective-permute-start.12
  152.1 12.5 %attend_back.3 = (bf16[2048,384]{1,0:T(8,128)(2,1)}, bf16[2048,384]{1,0:T(8,128)(2,1)}, bf16[2048,384]{1,0:T(8,128)(2,1)}) custom-call(s32[30,8]{1,0:T(8,128)S(1)} %select_reduce_fusion.key_at_ref, s32[30,8]{1,0:T(8,128)S(1)} %broadcast_select_fusion.22.bias_at_ref, s32[32]{0:T(128)S(1)} %pad_add_fusion.query_at_ref, ...), custom_call_target="tpu_custom_call" | custom-call | flops 15000000512 | bytes 6291456 | tf_op jit(solution)/shard_map/attend_back/pallas_call | solution.py:296
  167.8 12.2 %attend_back.4 = (bf16[2048,384]{1,0:T(8,128)(2,1)}, bf16[2048,384]{1,0:T(8,128)(2,1)}, bf16[2048,384]{1,0:T(8,128)(2,1)}) custom-call(s32[30,8]{1,0:T(8,128)S(1)} %select_reduce_fusion.key_at_ref, s32[30,8]{1,0:T(8,128)S(1)} %broadcast_select_fusion.22.bias_at_ref, ...), custom_call_target="tpu_custom_call", output_to_operand_aliasing={{0}: (11, {}), {1}: (12, {}), {2}: (13, {})} | custom-call | flops 15000000512 | bytes 6291456 | tf_op jit(solution)/shard_map/attend_back/pallas_call | solution.py:296
  184.3 12.4 %attend_back.5 = (bf16[2048,384]{1,0:T(8,128)(2,1)}, bf16[2048,384]{1,0:T(8,128)(2,1)}, bf16[2048,384]{1,0:T(8,128)(2,1)}) custom-call(s32[30,8]{1,0:T(8,128)S(1)} %select_reduce_fusion.key_at_ref, s32[30,8]{1,0:T(8,128)S(1)} %broadcast_select_fusion.22.bias_at_ref, ...), custom_call_target="tpu_custom_call", output_to_operand_aliasing={{0}: (11, {}), {1}: (12, {}), {2}: (13, {})} | custom-call | flops 15000000512 | bytes 6291456 | tf_op jit(solution)/shard_map/attend_back/pallas_call | solution.py:296
  198.9 1.8 fusion.4
  200.8 2.7 collective-permute-start.20
  203.8 8.8 %heads_products.1 = bf16[800,1152]{1,0:T(8,128)(2,1)} custom-call(bf16[2048,768]{1,0:T(8,128)(2,1)} %copy-done.26, bf16[2048,384]{1,0:T(8,128)(2,1)S(1)} %copy-done.8, bf16[2048,384]{1,0:T(8,128)(2,1)S(1)} %copy-done.9, bf16[2048,384]{1,0:T(8,128)(2,1)S(1)} %copy-done.12), custom_call_target="tpu_custom_call" | custom-call | flops 3774873600 | bytes 8388608 | tf_op jit(solution)/shard_map/heads_products/pallas_call | solution.py:657
  212.5 1.8 fusion.6
  215.5 3.2 add_convert_fusion.1
  221.2 10.8 %collective-permute-done.21 = bf16[144,768]{1,0:T(8,128)(2,1)} collective-permute-done((bf16[144,768]{1,0:T(8,128)(2,1)S(1)}, bf16[144,768]{1,0:T(8,128)(2,1)}, u32[]{:S(2)}, u32[]{:S(2)}) %collective-permute-start.21) | collective-permute-done | bytes 221216 | tf_op jit(solution)/shard_map/ppermute | solution.py:812
  233.3 2.0 add_convert_fusion.8
  235.3 1.7 add_convert_fusion.5
  239.5 1.7 add_convert_fusion.15
  242.4 9.8 %collective-permute-done.24 = bf16[144,768]{1,0:T(8,128)(2,1)S(1)} collective-permute-done((bf16[144,768]{1,0:T(8,128)(2,1)}, bf16[144,768]{1,0:T(8,128)(2,1)S(1)}, u32[]{:S(2)}, u32[]{:S(2)}) %collective-permute-start.24) | collective-permute-done | bytes 221216 | tf_op jit(solution)/shard_map/ppermute | solution.py:812
  253.2 1.8 collective-permute-start.28
  257.8 2.1 collective-permute-start.29
  259.9 1.9 add_convert_fusion.2
  261.8 4.8 %collective-permute-done.29 = bf16[100,1152]{1,0:T(8,128)(2,1)S(1)} collective-permute-done((bf16[100,1152]{1,0:T(8,128)(2,1)S(1)}, bf16[100,1152]{1,0:T(8,128)(2,1)S(1)}, u32[]{:S(2)}, u32[]{:S(2)}) %collective-permute-start.29) | collective-permute-done | bytes 230432 | tf_op jit(solution)/shard_map/ppermute | solution.py:812
  266.6 3.3 collective-permute-done.27
  271.0 2.1 collective-permute-start.32
  273.1 1.8 collective-permute-start.33
  278.0 7.8 %collective-permute-done.30 = bf16[100,1152]{1,0:T(8,128)(2,1)S(1)} collective-permute-done((bf16[100,1152]{1,0:T(8,128)(2,1)S(1)}, bf16[100,1152]{1,0:T(8,128)(2,1)S(1)}, u32[]{:S(2)}, u32[]{:S(2)}) %collective-permute-start.30) | collective-permute-done | bytes 230432 | tf_op jit(solution)/shard_map/ppermute | solution.py:812
  285.8 5.3 %collective-permute-done.33 = bf16[256,768]{1,0:T(8,128)(2,1)S(1)} collective-permute-done((bf16[256,768]{1,0:T(8,128)(2,1)S(1)}, bf16[256,768]{1,0:T(8,128)(2,1)S(1)}, u32[]{:S(2)}, u32[]{:S(2)}) %collective-permute-start.33) | collective-permute-done | bytes 393248 | tf_op jit(solution)/shard_map/ppermute | solution.py:812
  297.0 2.7 spread_outer.2.refs_0_
  299.8 13.3 %collective-permute-done.34 = bf16[100,1152]{1,0:T(8,128)(2,1)S(1)} collective-permute-done((bf16[100,1152]{1,0:T(8,128)(2,1)S(1)}, bf16[100,1152]{1,0:T(8,128)(2,1)S(1)}, u32[]{:S(2)}, u32[]{:S(2)}) %collective-permute-start.34) | collective-permute-done | bytes 230432 | tf_op jit(solution)/shard_map/ppermute | solution.py:812
  319.1 4.2 %spread_inner.2 = (f32[768,3072]{1,0:T(8,128)}, f32[768,768]{1,0:T(8,128)}) custom-call(s32[1]{0:T(128)} %bitcast.16.at_ref, bf16[1280,768]{1,0:T(8,128)(2,1)S(1)} %pad_maximum_fusion.1.first_ref, bf16[768,768]{1,0:T(8,128)(2,1)S(1)} %pad_maximum_fusion.8.second_ref.third_ref, bf16[768,768]{1,0:T(8,128)(2,1)S(1)} %pad_maximum_fusion.8.second_ref.third_ref), custom_call_target="tpu_custom_call" | custom-call | flops 1048576 | bytes 1024 | tf_op jit(solution)/shard_map/spread_inner/pallas_call | solution.py:730
  323.3 2.6 spread_outer.3
  326.0 2.6 collective-permute-done.42
  330.2 6.2 %spread_inner.3 = (f32[768,3072]{1,0:T(8,128)}, f32[768,768]{1,0:T(8,128)}) custom-call(s32[1]{0:T(128)} %bitcast.19.at_ref, bf16[1280,768]{1,0:T(8,128)(2,1)} %collective-permute-done.40.first_ref, bf16[768,768]{1,0:T(8,128)(2,1)S(1)} %collective-permute-done.41.second_ref.third_ref, ...), custom_call_target="tpu_custom_call", output_to_operand_aliasing={{0}: (4, {}), {1}: (5, {})} | custom-call | flops 1048576 | bytes 1024 | tf_op jit(solution)/shard_map/spread_inner/pallas_call | solution.py:730
  338.1 4.3 %collective-permute-done.43 = bf16[400,1152]{1,0:T(8,128)(2,1)S(1)} collective-permute-done((bf16[400,1152]{1,0:T(8,128)(2,1)S(1)}, bf16[400,1152]{1,0:T(8,128)(2,1)S(1)}, u32[]{:S(2)}, u32[]{:S(2)}) %collective-permute-start.43) | collective-permute-done | bytes 921632 | tf_op jit(solution)/shard_map/ppermute | solution.py:812
  344.9 2.3 spread_columns.2
  349.8 4.2 %spread_columns.3 = (f32[768,768]{1,0:T(8,128)}, f32[768,768]{1,0:T(8,128)}, f32[768,768]{1,0:T(8,128)}) custom-call(s32[1]{0:T(128)} %bitcast.19.at_ref, bf16[800,1152]{1,0:T(8,128)(2,1)} %collective-permute-done.44.pool_ref, f32[768,768]{1,0:T(8,128)} %get-tuple-element.317.refs_0_, ...), custom_call_target="tpu_custom_call", output_to_operand_aliasing={{0}: (2, {}), {1}: (3, {}), {2}: (4, {})} | custom-call | flops 1048576 | bytes 1024 | tf_op jit(solution)/shard_map/spread_columns/pallas_call | solution.py:683
  (349 shorter events, 80.3 us)
Async XLA Ops:
  3.3 20.8 %collective-permute-start = (bf16[512,768]{1,0:T(8,128)(2,1)}, bf16[512,768]{1,0:T(8,128)(2,1)}, u32[]{:S(2)}, u32[]{:S(2)}) collective-permute-start(bf16[512,768]{1,0:T(8,128)(2,1)} %get-tuple-element.344), channel_id=1, source_target_pairs={{0,16},{1,17},{2,18},{3,19},{4,20},{5,21},{6,22},{7,23},{8,24},{9,... | collective-permute-start | bytes 2359304 | tf_op jit(solution)/shard_map/ppermute | solution.py:812
  6.2 19.9 %collective-permute-start.1 = (bf16[512,768]{1,0:T(8,128)(2,1)S(1)}, bf16[512,768]{1,0:T(8,128)(2,1)}, u32[]{:S(2)}, u32[]{:S(2)}) collective-permute-start(bf16[512,768]{1,0:T(8,128)(2,1)S(1)} %get-tuple-element.343), channel_id=1, source_target_pairs={{0,8},{8,0},{16,24},{24,16},{1,9},{9,1},{17,25},{25,17},{2,10},{10... | collective-permute-start | bytes 2359304 | tf_op jit(solution)/shard_map/ppermute | solution.py:801
  17.7 12.4 %copy-start.18 = (bf16[768,1152]{1,0:T(8,128)(2,1)}, bf16[768,1152]{1,0:T(8,128)(2,1)S(1)}, u32[]{:S(2)}) copy-start(bf16[768,1152]{1,0:T(8,128)(2,1)S(1)} %pad_maximum_fusion.4) | copy-start | bytes 5308420
  26.1 2.5 collective-permute-start.2
  36.1 19.6 %collective-permute-start.3 = (bf16[512,768]{1,0:T(8,128)(2,1)S(1)}, bf16[512,768]{1,0:T(8,128)(2,1)S(1)}, u32[]{:S(2)}, u32[]{:S(2)}) collective-permute-start(bf16[512,768]{1,0:T(8,128)(2,1)S(1)} %dynamic-slice_bitcast_fusion), channel_id=1, source_target_pairs={{0,16},{1,17},{2,18},{3,19},{4,20},{5,21},{6,22},{7,23},{8,24},{9,... | collective-permute-start | bytes 2359304 | tf_op jit(solution)/shard_map/ppermute | solution.py:812
  55.8 2.4 collective-permute-start.4
  114.1 12.5 %collective-permute-start.8 = (bf16[1536,768]{1,0:T(8,128)(2,1)}, bf16[1536,768]{1,0:T(8,128)(2,1)}, u32[]{:S(2)}, u32[]{:S(2)}) collective-permute-start(bf16[1536,768]{1,0:T(8,128)(2,1)} %tall_product.4), channel_id=1, source_target_pairs={{0,8},{8,0},{16,24},{24,16},{1,9},{9,1},{17,25},{25,17},{2,10},{10... | collective-permute-start | bytes 7077896 | tf_op jit(solution)/shard_map/ppermute | solution.py:801
  120.3 15.0 %collective-permute-start.5 = (bf16[1536,768]{1,0:T(8,128)(2,1)}, bf16[1536,768]{1,0:T(8,128)(2,1)}, u32[]{:S(2)}, u32[]{:S(2)}) collective-permute-start(bf16[1536,768]{1,0:T(8,128)(2,1)} %wide_product.2), channel_id=1, source_target_pairs={{0,8},{8,0},{16,24},{24,16},{1,9},{9,1},{17,25},{25,17},{2,10},{10... | collective-permute-start | bytes 7077896 | tf_op jit(solution)/shard_map/ppermute | solution.py:801
  121.7 13.5 %collective-permute-start.7 = (bf16[128,768]{1,0:T(8,128)(2,1)S(1)}, bf16[128,768]{1,0:T(8,128)(2,1)S(1)}, u32[]{:S(2)}, u32[]{:S(2)}) collective-permute-start(bf16[128,768]{1,0:T(8,128)(2,1)S(1)} %pad_dynamic-slice_fusion.1), channel_id=1, source_target_pairs={{0,8},{8,0},{16,24},{24,16},{1,9},{9,1},{17,25},{25,17},{2,10},{10... | collective-permute-start | bytes 589832 | tf_op jit(solution)/shard_map/ppermute | solution.py:801
  124.0 11.2 %collective-permute-start.6 = (bf16[384,768]{1,0:T(8,128)(2,1)S(1)}, bf16[384,768]{1,0:T(8,128)(2,1)S(1)}, u32[]{:S(2)}, u32[]{:S(2)}) collective-permute-start(bf16[384,768]{1,0:T(8,128)(2,1)S(1)} %tall_product.5), channel_id=1, source_target_pairs={{0,8},{8,0},{16,24},{24,16},{1,9},{9,1},{17,25},{25,17},{2,10},{10... | collective-permute-start | bytes 1769480 | tf_op jit(solution)/shard_map/ppermute | solution.py:801
  124.4 27.7 %collective-permute-start.11 = (bf16[1024,384]{1,0:T(8,128)(2,1)}, bf16[1024,384]{1,0:T(8,128)(2,1)S(1)}, u32[]{:S(2)}, u32[]{:S(2)}) collective-permute-start(bf16[1024,384]{1,0:T(8,128)(2,1)} %get-tuple-element.217), channel_id=1, source_target_pairs={{0,8},{8,0},{16,24},{24,16},{1,9},{9,1},{17,25},{25,17},{2,10},{10... | collective-permute-start | bytes 2359304 | tf_op jit(solution)/shard_map/ppermute | solution.py:801
  132.5 13.4 %collective-permute-start.9 = (bf16[576,768]{1,0:T(8,128)(2,1)}, bf16[576,768]{1,0:T(8,128)(2,1)}, u32[]{:S(2)}, u32[]{:S(2)}) collective-permute-start(bf16[576,768]{1,0:T(8,128)(2,1)} %constant_dynamic-slice_fusion.10), channel_id=1, source_target_pairs={{0,16},{1,17},{2,18},{3,19},{4,20},{5,21},{6,22},{7,23},{8,9},{9,8... | collective-permute-start | bytes 2654216 | tf_op jit(solution)/shard_map/ppermute | solution.py:812
  135.3 9.0 %collective-permute-start.10 = (bf16[192,768]{1,0:T(8,128)(2,1)S(1)}, bf16[192,768]{1,0:T(8,128)(2,1)S(1)}, u32[]{:S(2)}, u32[]{:S(2)}) collective-permute-start(bf16[192,768]{1,0:T(8,128)(2,1)S(1)} %constant_dynamic-slice_fusion.9), channel_id=1, source_target_pairs={{0,2},{1,3},{2,0},{3,1},{4,6},{5,7},{6,4},{7,5},{8,10},{9,11},{10,... | collective-permute-start | bytes 884744 | tf_op jit(solution)/shard_map/ppermute | solution.py:812
  148.6 16.4 %collective-permute-start.12 = (bf16[640,768]{1,0:T(8,128)(2,1)S(1)}, bf16[640,768]{1,0:T(8,128)(2,1)S(1)}, u32[]{:S(2)}, u32[]{:S(2)}) collective-permute-start(bf16[640,768]{1,0:T(8,128)(2,1)S(1)} %constant_dynamic-slice_fusion.8), channel_id=1, source_target_pairs={{0,16},{1,17},{2,18},{3,19},{4,20},{5,21},{6,22},{7,23},{8,9},{9,8... | collective-permute-start | bytes 2949128 | tf_op jit(solution)/shard_map/ppermute | solution.py:812
  150.5 14.5 %collective-permute-start.13 = (bf16[384,768]{1,0:T(8,128)(2,1)S(1)}, bf16[384,768]{1,0:T(8,128)(2,1)S(1)}, u32[]{:S(2)}, u32[]{:S(2)}) collective-permute-start(bf16[384,768]{1,0:T(8,128)(2,1)S(1)} %constant_dynamic-slice_fusion.7), channel_id=1, source_target_pairs={{0,2},{1,3},{2,0},{3,1},{4,6},{5,7},{6,4},{7,5},{8,10},{9,11},{10,... | collective-permute-start | bytes 1769480 | tf_op jit(solution)/shard_map/ppermute | solution.py:812
  165.7 14.4 %collective-permute-start.14 = (bf16[608,768]{1,0:T(8,128)(2,1)S(1)}, bf16[608,768]{1,0:T(8,128)(2,1)S(1)}, u32[]{:S(2)}, u32[]{:S(2)}) collective-permute-start(bf16[608,768]{1,0:T(8,128)(2,1)S(1)} %constant_dynamic-slice_fusion.6), channel_id=1, source_target_pairs={{0,1},{1,0},{2,3},{3,2},{4,5},{5,4},{6,7},{7,6},{8,10},{9,11},{10,... | collective-permute-start | bytes 2801672 | tf_op jit(solution)/shard_map/ppermute | solution.py:812
  166.9 13.2 %collective-permute-start.15 = (bf16[288,768]{1,0:T(8,128)(2,1)S(1)}, bf16[288,768]{1,0:T(8,128)(2,1)S(1)}, u32[]{:S(2)}, u32[]{:S(2)}) collective-permute-start(bf16[288,768]{1,0:T(8,128)(2,1)S(1)} %constant_dynamic-slice_fusion.5), channel_id=1, source_target_pairs={{0,16},{1,17},{2,18},{3,19},{4,20},{5,21},{6,22},{7,23},{8,24},{9,... | collective-permute-start | bytes 1327112 | tf_op jit(solution)/shard_map/ppermute | solution.py:812
  180.5 16.2 %collective-permute-start.16 = (bf16[304,768]{1,0:T(8,128)(2,1)S(1)}, bf16[304,768]{1,0:T(8,128)(2,1)S(1)}, u32[]{:S(2)}, u32[]{:S(2)}) collective-permute-start(bf16[304,768]{1,0:T(8,128)(2,1)S(1)} %constant_dynamic-slice_fusion.4), channel_id=1, source_target_pairs={{0,2},{1,3},{2,0},{3,1},{4,6},{5,7},{6,4},{7,5},{8,24},{9,25},{10,... | collective-permute-start | bytes 1400840 | tf_op jit(solution)/shard_map/ppermute | solution.py:812
  182.2 14.5 %collective-permute-start.17 = (bf16[144,768]{1,0:T(8,128)(2,1)S(1)}, bf16[144,768]{1,0:T(8,128)(2,1)S(1)}, u32[]{:S(2)}, u32[]{:S(2)}) collective-permute-start(bf16[144,768]{1,0:T(8,128)(2,1)S(1)} %constant_dynamic-slice_fusion.3), channel_id=1, source_target_pairs={{0,1},{1,0},{2,3},{3,2},{4,5},{5,4},{6,7},{7,6},{8,9},{9,8},{10,11... | collective-permute-start | bytes 663560 | tf_op jit(solution)/shard_map/ppermute | solution.py:812
  183.8 12.9 %collective-permute-start.18 = (bf16[256,768]{1,0:T(8,128)(2,1)S(1)}, bf16[256,768]{1,0:T(8,128)(2,1)S(1)}, u32[]{:S(2)}, u32[]{:S(2)}) collective-permute-start(bf16[256,768]{1,0:T(8,128)(2,1)S(1)} %copy-done.45), channel_id=1, source_target_pairs={{0,16},{1,17},{2,18},{3,19},{4,20},{5,21},{6,22},{7,23},{8,24},{9,... | collective-permute-start | bytes 1179656 | tf_op jit(solution)/shard_map/ppermute | solution.py:812
  184.3 14.6 %copy-start.19 = (bf16[768,1152]{1,0:T(8,128)(2,1)S(1)}, bf16[768,1152]{1,0:T(8,128)(2,1)}, u32[]{:S(2)}) copy-start(bf16[768,1152]{1,0:T(8,128)(2,1)} %copy-done.18) | copy-start | bytes 5308420
  197.5 15.1 %collective-permute-start.19 = (bf16[256,768]{1,0:T(8,128)(2,1)}, bf16[256,768]{1,0:T(8,128)(2,1)S(1)}, u32[]{:S(2)}, u32[]{:S(2)}) collective-permute-start(bf16[256,768]{1,0:T(8,128)(2,1)} %get-tuple-element.263), channel_id=1, source_target_pairs={{0,16},{1,17},{2,18},{3,19},{4,20},{5,21},{6,22},{7,23},{8,24},{9,... | collective-permute-start | bytes 1179656 | tf_op jit(solution)/shard_map/ppermute | solution.py:812
  200.8 31.3 %collective-permute-start.20 = (bf16[304,768]{1,0:T(8,128)(2,1)S(1)}, bf16[304,768]{1,0:T(8,128)(2,1)}, u32[]{:S(2)}, u32[]{:S(2)}) collective-permute-start(bf16[304,768]{1,0:T(8,128)(2,1)S(1)} %add_convert_fusion.9), channel_id=1, source_target_pairs={{0,4},{1,5},{2,6},{3,7},{4,0},{5,1},{6,2},{7,3},{8,12},{9,13},{10,... | collective-permute-start | bytes 1400840 | tf_op jit(solution)/shard_map/ppermute | solution.py:812
  203.4 28.6 %collective-permute-start.21 = (bf16[144,768]{1,0:T(8,128)(2,1)S(1)}, bf16[144,768]{1,0:T(8,128)(2,1)}, u32[]{:S(2)}, u32[]{:S(2)}) collective-permute-start(bf16[144,768]{1,0:T(8,128)(2,1)S(1)} %add_convert_fusion.16), channel_id=1, source_target_pairs={{0,4},{1,5},{2,6},{3,7},{4,0},{5,1},{6,2},{7,3},{8,12},{9,13},{10,... | collective-permute-start | bytes 663560 | tf_op jit(solution)/shard_map/ppermute | solution.py:812
  214.5 17.5 %collective-permute-start.22 = (bf16[400,1152]{1,0:T(8,128)(2,1)S(1)}, bf16[400,1152]{1,0:T(8,128)(2,1)}, u32[]{:S(2)}, u32[]{:S(2)}) collective-permute-start(bf16[400,1152]{1,0:T(8,128)(2,1)S(1)} %constant_dynamic-slice_fusion.2), channel_id=1, source_target_pairs={{0,16},{1,17},{2,18},{3,19},{4,20},{5,21},{6,22},{7,23},{8,9},{9,8... | collective-permute-start | bytes 2764808 | tf_op jit(solution)/shard_map/ppermute | solution.py:812
  233.3 18.9 %collective-permute-start.26 = (bf16[1024,768]{1,0:T(8,128)(2,1)}, bf16[1024,768]{1,0:T(8,128)(2,1)}, u32[]{:S(2)}, u32[]{:S(2)}) collective-permute-start(bf16[1024,768]{1,0:T(8,128)(2,1)} %slice.157), channel_id=1, source_target_pairs={{0,8},{8,0},{16,24},{24,16},{1,9},{9,1},{17,25},{25,17},{2,10},{10... | collective-permute-start | bytes 4718600 | tf_op jit(solution)/shard_map/ppermute | solution.py:801
  235.3 16.9 %collective-permute-start.23 = (bf16[304,768]{1,0:T(8,128)(2,1)}, bf16[304,768]{1,0:T(8,128)(2,1)}, u32[]{:S(2)}, u32[]{:S(2)}) collective-permute-start(bf16[304,768]{1,0:T(8,128)(2,1)} %add_convert_fusion.8), channel_id=1, source_target_pairs={{0,2},{1,3},{2,0},{3,1},{4,6},{5,7},{6,4},{7,5},{8,24},{9,25},{10,... | collective-permute-start | bytes 1400840 | tf_op jit(solution)/shard_map/ppermute | solution.py:812
  238.7 13.5 %collective-permute-start.25 = (bf16[200,1152]{1,0:T(8,128)(2,1)}, bf16[200,1152]{1,0:T(8,128)(2,1)}, u32[]{:S(2)}, u32[]{:S(2)}) collective-permute-start(bf16[200,1152]{1,0:T(8,128)(2,1)} %constant_dynamic-slice_fusion.1), channel_id=1, source_target_pairs={{0,1},{1,0},{2,3},{3,2},{4,5},{5,4},{6,7},{7,6},{8,10},{9,11},{10,... | collective-permute-start | bytes 1382408 | tf_op jit(solution)/shard_map/ppermute | solution.py:812
  241.2 11.0 %collective-permute-start.24 = (bf16[144,768]{1,0:T(8,128)(2,1)}, bf16[144,768]{1,0:T(8,128)(2,1)S(1)}, u32[]{:S(2)}, u32[]{:S(2)}) collective-permute-start(bf16[144,768]{1,0:T(8,128)(2,1)} %add_convert_fusion.15), channel_id=1, source_target_pairs={{0,1},{1,0},{2,3},{3,2},{4,5},{5,4},{6,7},{7,6},{8,9},{9,8},{10,11... | collective-permute-start | bytes 663560 | tf_op jit(solution)/shard_map/ppermute | solution.py:812
  253.2 13.4 %collective-permute-start.28 = (bf16[288,768]{1,0:T(8,128)(2,1)S(1)}, bf16[288,768]{1,0:T(8,128)(2,1)S(1)}, u32[]{:S(2)}, u32[]{:S(2)}) collective-permute-start(bf16[288,768]{1,0:T(8,128)(2,1)S(1)} %pad_maximum_fusion.16), channel_id=1, source_target_pairs={{0,16},{1,17},{2,18},{3,19},{4,20},{5,21},{6,22},{7,23},{8,24},{9,... | collective-permute-start | bytes 1327112 | tf_op jit(solution)/shard_map/ppermute | solution.py:812
  256.3 13.6 %collective-permute-start.27 = (bf16[608,768]{1,0:T(8,128)(2,1)S(1)}, bf16[608,768]{1,0:T(8,128)(2,1)S(1)}, u32[]{:S(2)}, u32[]{:S(2)}) collective-permute-start(bf16[608,768]{1,0:T(8,128)(2,1)S(1)} %pad_maximum_fusion.10), channel_id=1, source_target_pairs={{0,1},{1,0},{2,3},{3,2},{4,5},{5,4},{6,7},{7,6},{8,10},{9,11},{10,... | collective-permute-start | bytes 2801672 | tf_op jit(solution)/shard_map/ppermute | solution.py:812
  257.8 8.8 %collective-permute-start.29 = (bf16[100,1152]{1,0:T(8,128)(2,1)S(1)}, bf16[100,1152]{1,0:T(8,128)(2,1)S(1)}, u32[]{:S(2)}, u32[]{:S(2)}) collective-permute-start(bf16[100,1152]{1,0:T(8,128)(2,1)S(1)} %constant_dynamic-slice_fusion), channel_id=1, source_target_pairs={{0,2},{1,3},{2,0},{3,1},{4,6},{5,7},{6,4},{7,5},{8,24},{9,25},{10,... | collective-permute-start | bytes 691208 | tf_op jit(solution)/shard_map/ppermute | solution.py:812
  270.4 21.5 %collective-permute-start.31 = (bf16[576,768]{1,0:T(8,128)(2,1)S(1)}, bf16[576,768]{1,0:T(8,128)(2,1)S(1)}, u32[]{:S(2)}, u32[]{:S(2)}) collective-permute-start(bf16[576,768]{1,0:T(8,128)(2,1)S(1)} %slice.183), channel_id=1, source_target_pairs={{0,16},{1,17},{2,18},{3,19},{4,20},{5,21},{6,22},{7,23},{8,9},{9,8... | collective-permute-start | bytes 2654216 | tf_op jit(solution)/shard_map/ppermute | solution.py:812
  271.0 14.9 %collective-permute-start.32 = (bf16[192,768]{1,0:T(8,128)(2,1)S(1)}, bf16[192,768]{1,0:T(8,128)(2,1)S(1)}, u32[]{:S(2)}, u32[]{:S(2)}) collective-permute-start(bf16[192,768]{1,0:T(8,128)(2,1)S(1)} %slice.184), channel_id=1, source_target_pairs={{0,2},{1,3},{2,0},{3,1},{4,6},{5,7},{6,4},{7,5},{8,10},{9,11},{10,... | collective-permute-start | bytes 884744 | tf_op jit(solution)/shard_map/ppermute | solution.py:812
  273.1 18.1 %collective-permute-start.33 = (bf16[256,768]{1,0:T(8,128)(2,1)S(1)}, bf16[256,768]{1,0:T(8,128)(2,1)S(1)}, u32[]{:S(2)}, u32[]{:S(2)}) collective-permute-start(bf16[256,768]{1,0:T(8,128)(2,1)S(1)} %slice.163), channel_id=1, source_target_pairs={{0,16},{1,17},{2,18},{3,19},{4,20},{5,21},{6,22},{7,23},{8,24},{9,... | collective-permute-start | bytes 1179656 | tf_op jit(solution)/shard_map/ppermute | solution.py:812
  275.0 10.8 %collective-permute-start.30 = (bf16[100,1152]{1,0:T(8,128)(2,1)S(1)}, bf16[100,1152]{1,0:T(8,128)(2,1)S(1)}, u32[]{:S(2)}, u32[]{:S(2)}) collective-permute-start(bf16[100,1152]{1,0:T(8,128)(2,1)S(1)} %add_convert_fusion.14), channel_id=1, source_target_pairs={{0,4},{1,5},{2,6},{3,7},{4,0},{5,1},{6,2},{7,3},{8,12},{9,13},{10,... | collective-permute-start | bytes 691208 | tf_op jit(solution)/shard_map/ppermute | solution.py:812
  292.3 20.9 %collective-permute-start.37 = (bf16[1152,768]{1,0:T(8,128)(2,1)S(1)}, bf16[1152,768]{1,0:T(8,128)(2,1)S(1)}, u32[]{:S(2)}, u32[]{:S(2)}) collective-permute-start(bf16[1152,768]{1,0:T(8,128)(2,1)S(1)} %pad_maximum_fusion.5.first_ref), channel_id=1, source_target_pairs={{0,8},{8,0},{16,24},{24,16},{1,9},{9,1},{17,25},{25,17},{2,10},{10... | collective-permute-start | bytes 5308424 | tf_op jit(solution)/shard_map/ppermute | solution.py:801
  292.4 20.7 %collective-permute-start.35 = (bf16[640,768]{1,0:T(8,128)(2,1)}, bf16[640,768]{1,0:T(8,128)(2,1)S(1)}, u32[]{:S(2)}, u32[]{:S(2)}) collective-permute-start(bf16[640,768]{1,0:T(8,128)(2,1)} %pad_maximum_fusion.9), channel_id=1, source_target_pairs={{0,16},{1,17},{2,18},{3,19},{4,20},{5,21},{6,22},{7,23},{8,9},{9,8... | collective-permute-start | bytes 2949128 | tf_op jit(solution)/shard_map/ppermute | solution.py:812
  294.7 18.4 %collective-permute-start.38 = (bf16[384,768]{1,0:T(8,128)(2,1)S(1)}, bf16[384,768]{1,0:T(8,128)(2,1)S(1)}, u32[]{:S(2)}, u32[]{:S(2)}) collective-permute-start(bf16[384,768]{1,0:T(8,128)(2,1)S(1)} %pad_maximum_fusion.14.second_ref), channel_id=1, source_target_pairs={{0,8},{8,0},{16,24},{24,16},{1,9},{9,1},{17,25},{25,17},{2,10},{10... | collective-permute-start | bytes 1769480 | tf_op jit(solution)/shard_map/ppermute | solution.py:801
  294.8 18.3 %collective-permute-start.36 = (bf16[384,768]{1,0:T(8,128)(2,1)S(1)}, bf16[384,768]{1,0:T(8,128)(2,1)S(1)}, u32[]{:S(2)}, u32[]{:S(2)}) collective-permute-start(bf16[384,768]{1,0:T(8,128)(2,1)S(1)} %copy-done.29), channel_id=1, source_target_pairs={{0,2},{1,3},{2,0},{3,1},{4,6},{5,7},{6,4},{7,5},{8,10},{9,11},{10,... | collective-permute-start | bytes 1769480 | tf_op jit(solution)/shard_map/ppermute | solution.py:812
  296.1 17.1 %copy-start.23 = (bf16[640,768]{1,0:T(8,128)(2,1)S(1)}, bf16[640,768]{1,0:T(8,128)(2,1)}, u32[]{:S(2)}) copy-start(bf16[640,768]{1,0:T(8,128)(2,1)} %pad_maximum_fusion.9) | copy-start | bytes 2949124
  296.1 17.0 %collective-permute-start.34 = (bf16[100,1152]{1,0:T(8,128)(2,1)S(1)}, bf16[100,1152]{1,0:T(8,128)(2,1)S(1)}, u32[]{:S(2)}, u32[]{:S(2)}) collective-permute-start(bf16[100,1152]{1,0:T(8,128)(2,1)S(1)} %add_convert_fusion.13), channel_id=1, source_target_pairs={{0,2},{1,3},{2,0},{3,1},{4,6},{5,7},{6,4},{7,5},{8,24},{9,25},{10,... | collective-permute-start | bytes 691208 | tf_op jit(solution)/shard_map/ppermute | solution.py:812
  314.9 13.7 %collective-permute-start.40 = (bf16[1280,768]{1,0:T(8,128)(2,1)S(1)}, bf16[1280,768]{1,0:T(8,128)(2,1)}, u32[]{:S(2)}, u32[]{:S(2)}) collective-permute-start(bf16[1280,768]{1,0:T(8,128)(2,1)S(1)} %pad_maximum_fusion.1.first_ref), channel_id=1, source_target_pairs={{0,8},{8,0},{16,24},{24,16},{1,9},{9,1},{17,25},{25,17},{2,10},{10... | collective-permute-start | bytes 5898248 | tf_op jit(solution)/shard_map/ppermute | solution.py:801
  316.2 12.4 %collective-permute-start.41 = (bf16[768,768]{1,0:T(8,128)(2,1)S(1)}, bf16[768,768]{1,0:T(8,128)(2,1)S(1)}, u32[]{:S(2)}, u32[]{:S(2)}) collective-permute-start(bf16[768,768]{1,0:T(8,128)(2,1)S(1)} %pad_maximum_fusion.8.second_ref.third_ref), channel_id=1, source_target_pairs={{0,8},{8,0},{16,24},{24,16},{1,9},{9,1},{17,25},{25,17},{2,10},{10... | collective-permute-start | bytes 3538952 | tf_op jit(solution)/shard_map/ppermute | solution.py:801
  317.2 11.4 %collective-permute-start.39 = (bf16[200,1152]{1,0:T(8,128)(2,1)S(1)}, bf16[200,1152]{1,0:T(8,128)(2,1)S(1)}, u32[]{:S(2)}, u32[]{:S(2)}) collective-permute-start(bf16[200,1152]{1,0:T(8,128)(2,1)S(1)} %pad_maximum_fusion.15), channel_id=1, source_target_pairs={{0,1},{1,0},{2,3},{3,2},{4,5},{5,4},{6,7},{7,6},{8,10},{9,11},{10,... | collective-permute-start | bytes 1382408 | tf_op jit(solution)/shard_map/ppermute | solution.py:812
  318.1 10.5 %collective-permute-start.42 = (bf16[256,768]{1,0:T(8,128)(2,1)S(1)}, bf16[256,768]{1,0:T(8,128)(2,1)S(1)}, u32[]{:S(2)}, u32[]{:S(2)}) collective-permute-start(bf16[256,768]{1,0:T(8,128)(2,1)S(1)} %slice.164), channel_id=1, source_target_pairs={{0,16},{1,17},{2,18},{3,19},{4,20},{5,21},{6,22},{7,23},{8,24},{9,... | collective-permute-start | bytes 1179656 | tf_op jit(solution)/shard_map/ppermute | solution.py:812
  328.9 13.5 %collective-permute-start.43 = (bf16[400,1152]{1,0:T(8,128)(2,1)S(1)}, bf16[400,1152]{1,0:T(8,128)(2,1)S(1)}, u32[]{:S(2)}, u32[]{:S(2)}) collective-permute-start(bf16[400,1152]{1,0:T(8,128)(2,1)S(1)} %pad_maximum_fusion.11), channel_id=1, source_target_pairs={{0,16},{1,17},{2,18},{3,19},{4,20},{5,21},{6,22},{7,23},{8,9},{9,8... | collective-permute-start | bytes 2764808 | tf_op jit(solution)/shard_map/ppermute | solution.py:812
  342.9 5.0 %collective-permute-start.44 = (bf16[800,1152]{1,0:T(8,128)(2,1)S(1)}, bf16[800,1152]{1,0:T(8,128)(2,1)}, u32[]{:S(2)}, u32[]{:S(2)}) collective-permute-start(bf16[800,1152]{1,0:T(8,128)(2,1)S(1)} %pad_maximum_fusion.3.pool_ref), channel_id=1, source_target_pairs={{0,8},{8,0},{16,24},{24,16},{1,9},{9,1},{17,25},{25,17},{2,10},{10... | collective-permute-start | bytes 5529608 | tf_op jit(solution)/shard_map/ppermute | solution.py:801
  (67 other events, 290.2 us)
where the time goes:
time: 361 us; the launch traced here: 354 us
  Pallas kernels  155 us (43%)
  waiting for transfers between devices  78.3 us (22%)
  starting transfers between devices  42.4 us (12%)
  local copies, waits for them, and re-layouts  33.1 us (9%)
  other arithmetic  30.1 us (8%)
  matrix products  12.7 us (4%)
    ppermute x31, waiting for transfers between devices, swap(): return lax.ppermute(value, ('seq', 'rows'), self.perm)  73.5 us
    pallas_call x1, Pallas kernels, feed_forward(): pl.pallas_call(partial(feed_forward_kernel, 1024, 256, len(context)), gri...  48.3 us
    ppermute x31, starting transfers between devices, swap(): return lax.ppermute(value, ('seq', 'rows'), self.perm)  40.7 us
    pallas_call x3, Pallas kernels, attend_back(): pl.pallas_call(partial(attend_back_kernel, heads, nb, abreast, len(pieces...  37.1 us
    pallas_call x1, Pallas kernels, attend(): pl.pallas_call(partial(attend_kernel, heads, nb, 2), grid=(1,), out_shape...  16.2 us
    pallas_call x4, Pallas kernels, spread_call(): pl.pallas_call(kernel, grid_spec=pltpu.PrefetchScalarGridSpec(num_scalar_...  15.7 us
    dot_general x4, matrix products, dot(): lax.dot_general(left, right, dims, preferred_element_type=jnp.float32)  12.7 us
    pallas_call x4, Pallas kernels, tall_product(): pl.pallas_call(tall_kernel, grid_spec=pltpu.PrefetchScalarGridSpec(num_sc...  11.8 us
  transfers between devices with their start and end apart: 45, of which 16 were waited for; matrix products, arithmetic and copies ran while one was open for 13% of the time, Pallas kernels for 28%

commit v1 on v0

--- a/solution.py
+++ b/solution.py
@@ -151,21 +151,26 @@
     key_at_ref,
     bias_at_ref,
     query_at_ref,
+    places_ref,
     q_ref,
     k_ref,
     v_ref,
     o_ref,
     lse_ref,
-    bias_ref,
     *rest,
 ):
-    dq_ref, dk_ref, dv_ref, dk_acc, dv_acc, delta_ref, g_ref = rest[-7:]
+    dq_ref, dk_ref, dv_ref, dk_acc, dv_acc, delta_ref, g_ref, bias_ref = rest[-8:]
     rows = nb * BLOCK // pieces
     for i in range(pieces):
         g_ref[i * rows : (i + 1) * rows, :] = rest[i][...]
     groups = head_groups(heads)
     diags = {n: diagonal(n, BLOCK) for _, n in groups}
+    inside = lax.broadcasted_iota(jnp.int32, (BLOCK, 2 * HEAD), 0)
+    for s in range(nb):
+        valid = places_ref[s] * BLOCK + inside < places_ref[nb]
+        bias_ref[s * BLOCK : (s + 1) * BLOCK, :] = jnp.where(valid, 0.0, NEG_FILL)
     every = nb * BLOCK
+    bias_ref[every:, :] = jnp.full_like(bias_ref[every:, :], NEG_FILL)
     dk_acc[every:, :] = jnp.zeros_like(dk_acc[every:, :])
     dv_acc[every:, :] = jnp.zeros_like(dv_acc[every:, :])
     scale = HEAD**-0.5
@@ -271,7 +276,7 @@
         ),
         in_specs=[SMEM] * 2 + list(specs) + [VMEM] * 2,
         out_specs=(VMEM, VMEM),
-        compiler_params=pltpu.CompilerParams(vmem_limit_bytes=48 << 20),
+        compiler_params=pltpu.CompilerParams(vmem_limit_bytes=30 << 20),
         cost_estimate=pl.CostEstimate(
             flops=20_000_000_000, bytes_accessed=8 << 20, transcendentals=0
         ),
@@ -280,7 +285,7 @@
 
 
 def attend_back(qkv, grads, context, lse, tables, heads, nb, held, at):
-    key_at, bias_at, query_at, bias, _, _ = tables
+    key_at, bias_at, query_at, places, _, _ = tables
     total = context.shape[1]
     width = heads * HEAD
     parts = total // width
@@ -291,15 +296,15 @@
     lse_spec = pl.BlockSpec((nb, 1, width), lambda i: (0, 0, at))
     out = jax.ShapeDtypeStruct((nb * BLOCK, total), jnp.bfloat16)
     out_spec = pl.BlockSpec((nb * BLOCK, width), lambda i: (0, at))
-    count = 3 + len(operands) + 2 + len(pieces)
+    count = 4 + len(operands) + 1 + len(pieces)
     abreast = 5 if (nb - 2) % 5 == 0 else 2
     return pl.pallas_call(
         partial(attend_back_kernel, heads, nb, abreast, len(pieces)),
         grid=(1,),
         out_shape=(out, out, out),
-        in_specs=[SMEM] * 3
+        in_specs=[SMEM] * 4
         + list(specs)
-        + [lse_spec, VMEM]
+        + [lse_spec]
         + list(piece_specs)
         + [pl.BlockSpec(memory_space=pl.ANY)] * len(held),
         out_specs=(out_spec,) * 3,
@@ -309,13 +314,14 @@
             pltpu.VMEM(((nb + 1) * BLOCK, width), jnp.float32),
             pltpu.VMEM((nb, 1, width), jnp.float32),
             pltpu.VMEM((nb * BLOCK, width), jnp.bfloat16),
+            pltpu.VMEM(((nb + 1) * BLOCK, 2 * HEAD), jnp.float32),
         ],
         compiler_params=pltpu.CompilerParams(vmem_limit_bytes=52 << 20),
         cost_estimate=pl.CostEstimate(
             flops=15_000_000_000, bytes_accessed=6 << 20, transcendentals=0
         ),
         name="attend_back",
-    )(key_at, bias_at, query_at, *operands, lse, bias, *pieces, *held)
+    )(key_at, bias_at, query_at, places, *operands, lse, *pieces, *held)
 
 
 def block_tables(block_of_slot, doc, random_blocks):
@@ -344,9 +350,8 @@
     lead_bias = bias.reshape(1, -1)
     task_bias = (index[..., None] * BLOCK + inside < doc) & allowed[..., None]
     task_bias = jnp.where(task_bias, 0.0, NEG_FILL).astype(jnp.float32).reshape(nb - 2, -1)
-    bias = jnp.concatenate([bias.reshape(-1), jnp.full((BLOCK,), NEG_FILL, jnp.float32)])
-    bias = jnp.broadcast_to(bias[:, None], (bias.shape[0], 2 * HEAD))
-    return key_at, bias_at, query_at, bias, task_bias, lead_bias
+    places = jnp.concatenate([block_of_slot, jnp.reshape(doc, (1,))])
+    return key_at, bias_at, query_at, places, task_bias, lead_bias
 
 
 TANH_SCALE = 0.7978845608028654
@@ -383,11 +388,12 @@
     *refs,
 ):
     context_refs, refs = refs[:pieces], refs[pieces:]
-    result_ref, first_ref, active_out_ref, d_inner_out_ref, d_outer_ref, d_attended_ref = refs[:6]
-    d_resid_ref, sums_ref, inner_sum_ref = refs[6:9]
-    d_context_refs, refs = refs[9 : 9 + pieces], refs[9 + pieces :]
+    result_refs, refs = refs[:3], refs[3:]
+    first_ref, active_out_ref, d_inner_out_ref, d_outer_ref, d_attended_ref = refs[:5]
+    d_resid_ref, sums_ref, inner_sum_ref = refs[5:8]
+    d_context_refs, refs = refs[8 : 8 + pieces], refs[8 + pieces :]
     w1_ref, w2_ref, active_ref, d_inner_ref, *refs = refs
-    slope_ref, held_ref, normal_ref, scale_ref, acc_ref, sems = refs
+    slope_ref, held_ref, normal_ref, scale_ref, result_ref, sems = refs
     cols = D // pieces
     first_step = pl.program_id(0) == 0
     tile = active_ref.shape[0]
@@ -408,30 +414,22 @@
 
     bo, g1, s1, b2, g2, s2 = [vec_ref[i : i + 1, :] for i in range(6)]
 
-    def each_rows(body):
-        def step(i, carry):
-            body(pl.ds(pl.multiple_of(i * few, few), few))
-            return carry
-
-        lax.fori_loop(0, tokens // few, step, 0)
-
-    def each_columns(body):
-        def step(i, carry):
-            body(pl.ds(pl.multiple_of(i * chunk, chunk), chunk))
-            return carry
-
-        lax.fori_loop(0, hidden // chunk, step, 0)
+    chunks = [slice(i, i + few) for i in range(0, tokens, few)]
+
+    col_chunks = [slice(i, i + chunk) for i in range(0, hidden, chunk)]
 
     def add_sum(row, values):
         sums_ref[row : row + 1, :] += jnp.sum(values, 0, keepdims=True)
 
-    for k, ref in enumerate(context_refs):
-        part = dot(ref[...], wo_ref[k * cols : (k + 1) * cols, :], NN)
-        acc_ref[...] = part if k == 0 else acc_ref[...] + part
-
-    @each_rows
-    def _(rows):
-        normal, scale = norm_rows(x_ref[rows, :].astype(full) + acc_ref[rows, :] + bo)
+    def add_context(rows):
+        parts = [
+            dot(ref[rows, :], wo_ref[k * cols : (k + 1) * cols, :], NN)
+            for k, ref in enumerate(context_refs)
+        ]
+        return sum(parts[1:], parts[0])
+
+    for rows, attended in [(rows, add_context(rows)) for rows in chunks]:
+        normal, scale = norm_rows(x_ref[rows, :].astype(full) + attended + bo)
         first = normal * g1 + s1
         normal_ref[rows, :] = normal
         scale_ref[rows, :] = jnp.broadcast_to(scale, (few, 128))
@@ -442,14 +440,13 @@
     def _():
         load_w1.wait()
 
-    @each_columns
-    def _(cols):
-        u = dot(first_ref[...], w1_ref[:, cols], NN) + b1_ref[:1, cols]
+    for cols_at, product in [(c, dot(first_ref[...], w1_ref[:, c], NN)) for c in col_chunks]:
+        u = product + b1_ref[:1, cols_at]
         square = u * u
         tanh = jnp.tanh(u * (TANH_SCALE + (TANH_SCALE * TANH_CUBE) * square))
         share = 0.5 * tanh + 0.5
-        active_ref[:, cols] = (u * share).astype(low)
-        slope_ref[:, cols] = share + (0.5 * u) * (1.0 - tanh * tanh) * (
+        active_ref[:, cols_at] = (u * share).astype(low)
+        slope_ref[:, cols_at] = share + (0.5 * u) * (1.0 - tanh * tanh) * (
             TANH_SCALE + (3 * TANH_SCALE * TANH_CUBE) * square
         )
 
@@ -459,11 +456,8 @@
     def _():
         load_w2.wait()
 
-    acc_ref[...] = dot(active_ref[...], w2_ref[...], NN)
-
-    @each_rows
-    def _(rows):
-        normal, scale = norm_rows(held_ref[rows, :] + acc_ref[rows, :] + b2)
+    for rows, outer in [(rows, dot(active_ref[rows, :], w2_ref[...], NN)) for rows in chunks]:
+        normal, scale = norm_rows(held_ref[rows, :] + outer + b2)
         result_ref[rows, :] = (normal * g2 + s2).astype(low)
         own = pl.program_id(0) == 0
         cot = jnp.where(own, cot_own_ref[0, rows, :], cot_came_ref[rows, :]).astype(full)
@@ -475,18 +469,25 @@
         add_sum(4, cot * normal)
         add_sum(5, cot)
 
-    @each_columns
-    def _(cols):
-        d_inner = (dot(d_outer_ref[...], w2_ref[cols, :], NT) * slope_ref[:, cols]).astype(low)
-        d_inner_ref[:, cols] = d_inner
-        inner_sum_ref[:1, cols] += jnp.sum(d_inner.astype(full), 0, keepdims=True)
+    @pl.when(first_step)
+    def _():
+        result_refs[0][...] = result_ref[...]
+
+    @pl.when(jnp.logical_not(first_step))
+    def _():
+        result_refs[1][...] = result_ref[: tile // 2, :]
+        result_refs[2][...] = result_ref[tile // 2 :, :]
+
+    for cols_at, product in [
+        (c, dot(d_outer_ref[...], w2_ref[c, :], NT)) for c in col_chunks
+    ]:
+        d_inner = (product * slope_ref[:, cols_at]).astype(low)
+        d_inner_ref[:, cols_at] = d_inner
+        inner_sum_ref[:1, cols_at] += jnp.sum(d_inner.astype(full), 0, keepdims=True)
 
     store_d_inner.start()
-    acc_ref[...] = dot(d_inner_ref[...], w1_ref[...], NT)
-
-    @each_rows
-    def _(rows):
-        d_first = held_ref[rows, :] + acc_ref[rows, :]
+    for rows, back in [(rows, dot(d_inner_ref[rows, :], w1_ref[...], NT)) for rows in chunks]:
+        d_first = held_ref[rows, :] + back
         normal = normal_ref[rows, :]
         add_sum(1, d_first * normal)
         add_sum(2, d_first)
@@ -495,9 +496,10 @@
         d_attended = d_resid.astype(low)
         d_attended_ref[rows, :] = d_attended
         add_sum(0, d_attended.astype(full))
-
-    for k, ref in enumerate(d_context_refs):
-        ref[...] = dot(d_attended_ref[...], wo_ref[k * cols : (k + 1) * cols, :], NT).astype(low)
+    for rows in chunks:
+        for k, ref in enumerate(d_context_refs):
+            part = dot(d_attended_ref[rows, :], wo_ref[k * cols : (k + 1) * cols, :], NT)
+            ref[rows, :] = part.astype(low)
     store_active.wait()
     store_d_inner.wait()
 
@@ -509,6 +511,7 @@
     row = pl.BlockSpec((tile, D), lambda i, at: (i, 0))
     part = pl.BlockSpec((tile, cols), lambda i, at: (i, 0))
     there = pl.BlockSpec(memory_space=pl.ANY)
+    shards = (tile, tile // 2, tile // 2)
     once = pl.Buffered(1)
     whole = lambda a: pl.BlockSpec(a.shape, lambda i, at: (0,) * a.ndim, pipeline_mode=once)
     shape = jax.ShapeDtypeStruct
@@ -523,7 +526,8 @@
             ]
             + [whole(cot_came), whole(wo), there, there, whole(vec), whole(b1)]
             + [part] * len(context),
-            out_specs=[row, row, there, there, row, row, row]
+            out_specs=[pl.BlockSpec((n, D), lambda i, at: (0, 0)) for n in shards]
+            + [row, there, there, row, row, row]
             + [pl.BlockSpec((8, n), lambda i, at: (0, 0)) for n in (D, hidden)]
             + [part] * len(context),
             scratch_shapes=[
@@ -535,12 +539,12 @@
                 pltpu.VMEM((tile, D), full),
                 pltpu.VMEM((tile, D), full),
                 pltpu.VMEM((tile, 128), full),
-                pltpu.VMEM((tile, D), full),
+                pltpu.VMEM((tile, D), low),
                 pltpu.SemaphoreType.DMA((4,)),
             ],
         ),
-        out_shape=[
-            shape((tokens, D), low),
+        out_shape=[shape((n, D), low) for n in shards]
+        + [
             shape((tokens, D), low),
             shape((tokens, hidden), low),
             shape((tokens, hidden), low),
@@ -661,12 +665,51 @@
         out_specs=pl.BlockSpec((rows, cols), lambda i: (0, i)),
         out_shape=jax.ShapeDtypeStruct((rows, 3 * cols), jnp.bfloat16),
         scratch_shapes=[pltpu.VMEM((rows, tokens), jnp.bfloat16)],
-        compiler_params=pltpu.CompilerParams(vmem_limit_bytes=48 << 20),
+        compiler_params=pltpu.CompilerParams(vmem_limit_bytes=62 << 20),
         cost_estimate=pl.CostEstimate(
             flops=6 * tokens * rows * cols, bytes_accessed=8 << 20, transcendentals=0
         ),
         name="heads_products",
     )(x, d_query, d_key, d_value)
+
+
+def inputs_kernel(at_ref, d_query_ref, d_key_ref, d_value_ref, wq_ref, wk_ref, wv_ref, *out_refs):
+    total = dot(d_query_ref[...], wq_ref[...], NT)
+    total = total + dot(d_key_ref[...], wk_ref[...], NT)
+    total = (total + dot(d_value_ref[...], wv_ref[...], NT)).astype(jnp.bfloat16)
+    per = pl.num_programs(0) // len(out_refs)
+    for k, ref in enumerate(out_refs):
+
+        @pl.when(pl.program_id(0) // per == k)
+        def _():
+            ref[...] = total
+
+
+def inputs_products(grads, weights, at, count):
+    tokens, cols = grads[0].shape
+    tile = 512
+    per = tokens // count // tile
+    part = pl.BlockSpec((tile, cols), lambda i, at: (i, 0))
+    weight = pl.BlockSpec((D, cols), lambda i, at: (0, at[0]), pipeline_mode=pl.Buffered(1))
+
+    def place(k):
+        return pl.BlockSpec((tile, D), lambda i, at: (jnp.clip(i - k * per, 0, per - 1), 0))
+
+    return pl.pallas_call(
+        inputs_kernel,
+        grid_spec=pltpu.PrefetchScalarGridSpec(
+            num_scalar_prefetch=1,
+            grid=(count * per,),
+            in_specs=[part] * 3 + [weight] * 3,
+            out_specs=[place(k) for k in range(count)],
+        ),
+        out_shape=[jax.ShapeDtypeStruct((tokens // count, D), jnp.bfloat16)] * count,
+        compiler_params=pltpu.CompilerParams(vmem_limit_bytes=60 << 20),
+        cost_estimate=pl.CostEstimate(
+            flops=24_000_000_000, bytes_accessed=8 << 20, transcendentals=0
+        ),
+        name="inputs_products",
+    )(jnp.reshape(at, (1,)).astype(jnp.int32), *grads, *weights)
 
 
 def spread_heads_kernel(at_ref, pool_ref, *refs):
@@ -1006,7 +1049,8 @@
     def my_cols(weight):
         return lax.dynamic_slice_in_dim(weight, at * cols, cols, weight.ndim - 1)
 
-    w_qkv = jnp.concatenate([my_cols(w) for w in (query_weight, key_weight, value_weight)], 1)
+    weights = (query_weight, key_weight, value_weight)
+    w_qkv = jnp.concatenate([my_cols(w) for w in weights], 1)
     b_qkv = jnp.concatenate(
         [my_cols(query_bias), jnp.zeros((cols,), low), my_cols(value_bias)]
     ).astype(full)
@@ -1040,20 +1084,11 @@
     context = [heads_context] + [
         near.send(heads_context[k * tokens : (k + 1) * tokens], k) for k in range(1, half)
     ]
-    (
-        result,
-        first_low,
-        active,
-        d_inner,
-        d_outer,
-        d_attended,
-        d_resid,
-        sums,
-        inner_sum,
-        *d_context,
-    ) = feed_forward(
+    values = feed_forward(
         mine, x_all, cotangent, cot_came, context, wo, inner_weight, outer_weight, vec, b1
     )
+    result, result_half, values = values[0], list(values[1:3]), values[3:]
+    first_low, active, d_inner, d_outer, d_attended, d_resid, sums, inner_sum, *d_context = values
     heads_grad = [d_context[0]] + [near.send(d_context[k], half - k) for k in range(1, half)]
 
     packed = jnp.concatenate([sums[:6].reshape(-1), inner_sum[0]]).reshape(-1, D)
@@ -1119,7 +1154,6 @@
 
     steps = cols // 128 if cols % 128 == 0 else 1
     d_qkv = ()
-    result_half = [result[width : width + width // 2], result[width + width // 2 :]]
     result_came = []
     for k in range(steps):
         chain = first if first.parts else rest
@@ -1146,7 +1180,7 @@
         first.start()
         first.finish()
     sums_at_last = first.steps.pop(0)
-    last_came = sums_at_last.start(first.parts[:1]) + sums_at_last.start(first.parts[1:])
+    last_came = sums_at_last.start(first.parts[1:])
     result_half[1:], d_query = in_step([*result_half[1:], d_query])[:-1], d_query
     result_came += [far.swap(piece) for piece in result_half[len(result_came) :]]
     if cols % 128 == 0:
@@ -1157,16 +1191,24 @@
             jnp.concatenate([dot(x_all, d, TN), total], 0) for d, total in zip(d_qkv, sums_of)
         ]
         heads_part = jnp.concatenate(heads_part, 1).astype(low)
-    heads_part, d_query, *result_came = in_step([heads_part, d_query] + result_came)
+    heads_part, d_query, d_key, d_value, *came = in_step(
+        [heads_part, d_query, d_key, d_value] + last_came + result_came
+    )
+    last_came, result_came = came[:1], came[1:]
+    first.parts[0], heads_part = in_step([first.parts[0], heads_part])
 
     second = Chain([heads_part], [HalveStep([main[i]]) for i in range(3)])
     second.steps += [SumStep(pair) for pair in last]
     second.steps += [JoinStep([main[i]]) for i in (2, 1, 0)]
     second.start()
-    wq, wk, wv = (w_qkv[:, i * cols : (i + 1) * cols] for i in range(3))
-    d_part = (dot(d_query, wq, NT) + dot(d_key, wk, NT) + dot(d_value, wv, NT)).astype(low)
-    result = from_rows(result[:width], jnp.concatenate(result_came, 0))
-    d_part, result, *came = in_step([d_part, result] + last_came + second.came)
+    last_came = sums_at_last.start(first.parts[:1]) + last_came
+    if cols % 128 == 0:
+        d_parts = list(inputs_products((d_query, d_key, d_value), weights, at, half))
+    else:
+        parts = zip((d_query, d_key, d_value), (my_cols(w) for w in weights))
+        d_parts = sum(dot(d, w, NT) for d, w in parts).astype(low)
+        d_parts = cut(d_parts, [tokens] * half)
+    d_parts[0], *came = in_step([d_parts[0]] + last_came + second.came)
     first.parts, second.came = sums_at_last.finish(first.parts, came[:2]), came[2:]
     second.finish()
 
@@ -1182,15 +1224,16 @@
 
     second.start()
     first.start()
-    d_came = [near.send(d_part[k * tokens : (k + 1) * tokens], k) for k in range(1, half)]
+    d_came = [near.send(d_parts[k], k) for k in range(1, half)]
     d_came = together(*d_came)
     second.start()
     first.start()
-    d_input = d_resid + d_part[:tokens].astype(full)
+    d_input = d_resid + d_parts[0].astype(full)
     for value in d_came:
         d_input = d_input + value.astype(full)
     d_input = d_input.astype(low)
-    (d_input,) = together(d_input)
+    result = from_rows(result, jnp.concatenate(result_came, 0))
+    d_input, result = together(d_input, result)
     for _ in last[:-1]:
         second.step()
     second.start()
@@ -1199,9 +1242,8 @@
     inner = Chain([pieces[1], pieces[3]], [JoinStep([main[0], side[0]])])
     outer.start()
     d_input_came = [far.swap(d_input[width : width + width // 2])]
-    outer.came, inner.parts, d_input_came = (
-        lambda v: (v[:2], v[2:4], v[4:])
-    )(together(*outer.came, *inner.parts, *d_input_came))
+    values = together(*outer.came, *inner.parts, *d_input_came)
+    outer.came, inner.parts, d_input_came = values[:2], values[2:4], values[4:]
     outer.finish()
     second.start()
     inner.start()

time: 361 us -> 350 us (0.970); the launches traced: 354 us -> 347 us
  Pallas kernels: 155 us -> 165 us
  matrix products: 12.7 us -> 4.49 us
  other arithmetic: 30.1 us -> 25.5 us
  local copies, waits for them, and re-layouts: 33.1 us -> 29 us
    pallas_call x0 -> x1, Pallas kernels: none -> 9.1 us  [inputs_products(): pl.pallas_call(inputs_kernel, grid_spec=pltpu.PrefetchScalarGridSpec(num_...]
    dot_general x4 -> x1, matrix products: 12.7 us -> 4.49 us  [dot(): lax.dot_general(left, right, dims, preferred_element_type=jnp.float32)]
    unnamed x141 -> x143, local copies, waits for them, and re-layouts: 11.3 us -> 11.9 us
  transfers between devices with their start and end apart: 45 -> 45, of which waited for: 16 -> 16; matrix products, arithmetic and copies ran while one was open for 13% -> 9% of each run, Pallas kernels for 28% -> 30%
where the time goes in v1:
time: 350 us; the launch traced here: 347 us
  Pallas kernels  165 us (47%)
  waiting for transfers between devices  80.8 us (23%)
  starting transfers between devices  40.7 us (12%)
  local copies, waits for them, and re-layouts  29 us (8%)
  other arithmetic  25.5 us (7%)
  matrix products  4.49 us (1%)
    ppermute x31, waiting for transfers between devices, swap(): return lax.ppermute(value, ('seq', 'rows'), self.perm)  74.8 us
    pallas_call x1, Pallas kernels, feed_forward(): pl.pallas_call(partial(feed_forward_kernel, 1024, 256, len(context)), gri...  50.1 us
    ppermute x31, starting transfers between devices, swap(): return lax.ppermute(value, ('seq', 'rows'), self.perm)  39 us
    pallas_call x3, Pallas kernels, attend_back(): pl.pallas_call(partial(attend_back_kernel, heads, nb, abreast, len(pieces...  36.4 us
    pallas_call x4, Pallas kernels, spread_call(): pl.pallas_call(kernel, grid_spec=pltpu.PrefetchScalarGridSpec(num_scalar_...  15.5 us
    pallas_call x1, Pallas kernels, attend(): pl.pallas_call(partial(attend_kernel, heads, nb, 2), grid=(1,), out_shape...  14.6 us
    unnamed x143, local copies, waits for them, and re-layouts  11.9 us
    pallas_call x4, Pallas kernels, tall_product(): pl.pallas_call(tall_kernel, grid_spec=pltpu.PrefetchScalarGridSpec(num_sc...  11.7 us
  transfers between devices with their start and end apart: 45, of which 16 were waited for; matrix products, arithmetic and copies ran while one was open for 9% of the time, Pallas kernels for 30%

profile of v1, /device:TPU:0, one launch (start us, length us, event | category | flops | bytes accessed | tf_op | source)
XLA Modules:
  0.0 347.5 jit_solution(4520339509443146382)
XLA Ops:
  0.8 2.4 dynamic-slice_bitcast_fusion.1
  3.2 2.9 collective-permute-start
  11.5 1.5 constant_dynamic-slice_fusion.13
  17.3 6.7 %collective-permute-done = bf16[512,768]{1,0:T(8,128)(2,1)} collective-permute-done((bf16[512,768]{1,0:T(8,128)(2,1)}, bf16[512,768]{1,0:T(8,128)(2,1)}, u32[]{:S(2)}, u32[]{:S(2)}) %collective-permute-start) | collective-permute-done | bytes 786464 | tf_op jit(solution)/shard_map/ppermute | solution.py:855
  24.7 2.5 collective-permute-done.2
  27.1 1.5 pad_maximum_fusion.x_ref
  28.8 4.5 %add_convert_fusion.q_ref.k_ref.v_ref = bf16[2048,1152]{1,0:T(8,128)(2,1)S(1)} fusion(bf16[2048,768]{1,0:T(8,128)(2,1)S(1)} %pad_maximum_fusion.x_ref, bf16[768,1152]{1,0:T(8,128)(2,1)S(1)} %pad_maximum_fusion.4, f32[1152]{0:T(1024)S(1)} %maximum_convert_fusion), kind=kOutput, calls=%fused_computation | convolution fusion | flops 3628597248 | bytes 9638400 | tf_op jit(solution)/shard_map/dot_general | solution.py:29
  33.3 1.8 collective-permute-start.3
  35.1 14.6 %attend.1 = (bf16[2048,384]{1,0:T(8,128)(2,1)S(1)}, f32[32,1,384]{2,1,0:T(1,128)S(1)}) custom-call(s32[30,8]{1,0:T(8,128)S(1)} %select_reduce_fusion.key_at_ref, s32[32]{0:T(128)S(1)} %pad_add_fusion.query_at_ref, bf16[2048,1152]{1,0:T(8,128)(2,1)S(1)} %add_convert_fusion.q_ref.k_ref.v_ref, bf16[2048,1152]{1,0:T(8,128)(2,1)S(1)} %add_convert_fusion.q_ref.k_ref.v_ref, ...), custom_call_target="tpu_custom_call" | custom-call | flops 20000000000 | bytes 8388608 | tf_op jit(solution)/shard_map/attend/pallas_call | solution.py:270
  50.3 2.6 collective-permute-done.3.cot_came_ref
  53.1 2.3 collective-permute-done.4.refs_1_.left_ref
  56.3 50.1 %feed_forward.1 = (bf16[512,768]{1,0:T(8,128)(2,1)}, bf16[256,768]{1,0:T(8,128)(2,1)}, bf16[256,768]{1,0:T(8,128)(2,1)}, bf16[1024,768]{1,0:T(8,128)(2,1)}, bf16...) custom-call(s32[1]{0:T(128)} %bitcast.14.mine_ref, ...), custom_call_target="tpu_custom_call" | custom-call | flops 49999998976 | bytes 41943040 | tf_op jit(solution)/shard_map/feed_forward/pallas_call | solution.py:518
  107.8 5.4 %tall_product.4 = bf16[1536,768]{1,0:T(8,128)(2,1)} custom-call(s32[1]{0:T(128)} %bitcast.15.at_ref, bf16[1024,3072]{1,0:T(8,128)(2,1)} %get-tuple-element.203.left_ref, bf16[1024,768]{1,0:T(8,128)(2,1)S(1)} %copy-done.4), custom_call_target="tpu_custom_call" | custom-call | flops 2415919104 | bytes 8388608 | tf_op jit(solution)/shard_map/tall_product/pallas_call | solution.py:594
  113.4 5.9 %wide_product.2 = bf16[1536,768]{1,0:T(8,128)(2,1)} custom-call(s32[1]{0:T(128)} %bitcast.15.at_ref, bf16[1024,768]{1,0:T(8,128)(2,1)S(1)} %copy-done.2, bf16[1024,3072]{1,0:T(8,128)(2,1)} %get-tuple-element.208.right_ref), custom_call_target="tpu_custom_call" | custom-call | flops 2415919104 | bytes 8388608 | tf_op jit(solution)/shard_map/wide_product/pallas_call | solution.py:619
  123.7 4.7 %tall_product.6 = bf16[1536,768]{1,0:T(8,128)(2,1)S(1)} custom-call(s32[1]{0:T(128)} %bitcast.16.at_ref, bf16[1024,3072]{1,0:T(8,128)(2,1)} %get-tuple-element.203.left_ref, bf16[1024,768]{1,0:T(8,128)(2,1)S(1)} %copy-done.5, bf16[1536,768]{1,0:T(8,128)(2,1)} %collective-permute-done.8.refs_0_), custom_call_target="tpu_custom_call" | custom-call | flops 2415919104 | bytes 8388608 | tf_op jit(solution)/shard_map/tall_product/pallas_call | solution.py:594
  130.7 1.7 collective-permute-start.9
  134.9 1.7 collective-permute-start.10
  136.6 5.1 %wide_product.3 = bf16[1536,768]{1,0:T(8,128)(2,1)S(1)} custom-call(s32[1]{0:T(128)} %bitcast.16.at_ref, bf16[1024,768]{1,0:T(8,128)(2,1)S(1)} %copy-done.3, bf16[1024,3072]{1,0:T(8,128)(2,1)} %get-tuple-element.208.right_ref, bf16[1536,768]{1,0:T(8,128)(2,1)} %collective-permute-done.5.refs_0_), custom_call_target="tpu_custom_call" | custom-call | flops 2415919104 | bytes 8388608 | tf_op jit(solution)/shard_map/wide_product/pallas_call | solution.py:619
  147.2 1.7 collective-permute-start.12
  149.0 1.7 collective-permute-start.13
  150.7 12.4 %attend_back.3 = (bf16[2048,384]{1,0:T(8,128)(2,1)}, bf16[2048,384]{1,0:T(8,128)(2,1)}, bf16[2048,384]{1,0:T(8,128)(2,1)}) custom-call(s32[30,8]{1,0:T(8,128)S(1)} %select_reduce_fusion.key_at_ref, s32[30,8]{1,0:T(8,128)S(1)} %copy-done.16, s32[32]{0:T(128)S(1)} %copy-done.19, s32[33]{0:T(128)S(1)} %copy-done.17, bf16[2048,1152]{1,0:T(8,128)(2,1)} %copy-done.20, ...), custom_call_target="tpu_custom_call" | custom-call | flops 15000000512 | bytes 6291456 | tf_op jit(solution)/shard_map/attend_back/pallas_call | solution.py:301
  166.6 12.0 %attend_back.4 = (bf16[2048,384]{1,0:T(8,128)(2,1)}, bf16[2048,384]{1,0:T(8,128)(2,1)}, bf16[2048,384]{1,0:T(8,128)(2,1)}) custom-call(s32[30,8]{1,0:T(8,128)S(1)} %select_reduce_fusion.key_at_ref, s32[30,8]{1,0:T(8,128)S(1)} %copy-done.16, s32[32]{0:T(128)S(1)} %copy-done.19, ...), custom_call_target="tpu_custom_call", output_to_operand_aliasing={{0}: (11, {}), {1}: (12, {}), {2}: (13, {})} | custom-call | flops 15000000512 | bytes 6291456 | tf_op jit(solution)/shard_map/attend_back/pallas_call | solution.py:301
  179.0 1.6 collective-permute-start.16
  182.7 12.0 %attend_back.5 = (bf16[2048,384]{1,0:T(8,128)(2,1)}, bf16[2048,384]{1,0:T(8,128)(2,1)}, bf16[2048,384]{1,0:T(8,128)(2,1)}) custom-call(s32[30,8]{1,0:T(8,128)S(1)} %select_reduce_fusion.key_at_ref, s32[30,8]{1,0:T(8,128)S(1)} %copy-done.16, s32[32]{0:T(128)S(1)} %copy-done.19, ...), custom_call_target="tpu_custom_call", output_to_operand_aliasing={{0}: (11, {}), {1}: (12, {}), {2}: (13, {})} | custom-call | flops 15000000512 | bytes 6291456 | tf_op jit(solution)/shard_map/attend_back/pallas_call | solution.py:301
  194.9 1.5 collective-permute-start.20
  196.4 2.6 collective-permute-start.19
  199.0 9.9 %heads_products.1 = bf16[800,1152]{1,0:T(8,128)(2,1)} custom-call(bf16[2048,768]{1,0:T(8,128)(2,1)} %copy-done.30, bf16[2048,384]{1,0:T(8,128)(2,1)} %get-tuple-element.278.d_query_ref, bf16[2048,384]{1,0:T(8,128)(2,1)} %get-tuple-element.279.d_key_ref, bf16[2048,384]{1,0:T(8,128)(2,1)} %get-tuple-element.280.d_value_ref), custom_call_target="tpu_custom_call" | custom-call | flops 3774873600 | bytes 8388608 | tf_op jit(solution)/shard_map/heads_products/pallas_call | solution.py:661
  211.9 9.1 %inputs_products.1 = (bf16[1024,768]{1,0:T(8,128)(2,1)}, bf16[1024,768]{1,0:T(8,128)(2,1)}) custom-call(s32[1]{0:T(128)} %bitcast.16.at_ref, bf16[2048,384]{1,0:T(8,128)(2,1)} %get-tuple-element.278.d_query_ref, bf16[2048,384]{1,0:T(8,128)(2,1)} %get-tuple-element.279.d_key_ref, bf16[2048,384]{1,0:T(8,128)(2,1)} %get-tuple-element.280.d_value_ref, ...), custom_call_target="tpu_custom_call" | custom-call | flops 24000000000 | bytes 8388608 | tf_op jit(solution)/shard_map/inputs_products/pallas_call | solution.py:698
  221.0 12.1 %collective-permute-done.21 = bf16[304,768]{1,0:T(8,128)(2,1)S(1)} collective-permute-done((bf16[304,768]{1,0:T(8,128)(2,1)S(1)}, bf16[304,768]{1,0:T(8,128)(2,1)S(1)}, u32[]{:S(2)}, u32[]{:S(2)}) %collective-permute-start.21) | collective-permute-done | bytes 466976 | tf_op jit(solution)/shard_map/ppermute | solution.py:855
  234.6 1.7 collective-permute-start.25
  239.7 8.2 %collective-permute-done.24 = bf16[144,768]{1,0:T(8,128)(2,1)S(1)} collective-permute-done((bf16[144,768]{1,0:T(8,128)(2,1)S(1)}, bf16[144,768]{1,0:T(8,128)(2,1)S(1)}, u32[]{:S(2)}, u32[]{:S(2)}) %collective-permute-start.24) | collective-permute-done | bytes 221216 | tf_op jit(solution)/shard_map/ppermute | solution.py:855
  249.5 1.7 collective-permute-start.27
  251.7 2.0 add_convert_fusion.1
  253.7 6.5 %collective-permute-done.29 = bf16[100,1152]{1,0:T(8,128)(2,1)S(1)} collective-permute-done((bf16[100,1152]{1,0:T(8,128)(2,1)S(1)}, bf16[100,1152]{1,0:T(8,128)(2,1)S(1)}, u32[]{:S(2)}, u32[]{:S(2)}) %collective-permute-start.29) | collective-permute-done | bytes 230432 | tf_op jit(solution)/shard_map/ppermute | solution.py:855
  260.2 2.9 collective-permute-done.27
  266.2 2.5 collective-permute-start.30
  270.5 8.7 %collective-permute-done.30 = bf16[100,1152]{1,0:T(8,128)(2,1)S(1)} collective-permute-done((bf16[100,1152]{1,0:T(8,128)(2,1)S(1)}, bf16[100,1152]{1,0:T(8,128)(2,1)S(1)}, u32[]{:S(2)}, u32[]{:S(2)}) %collective-permute-start.30) | collective-permute-done | bytes 230432 | tf_op jit(solution)/shard_map/ppermute | solution.py:855
  279.3 5.8 %collective-permute-done.33 = bf16[256,768]{1,0:T(8,128)(2,1)S(1)} collective-permute-done((bf16[256,768]{1,0:T(8,128)(2,1)S(1)}, bf16[256,768]{1,0:T(8,128)(2,1)S(1)}, u32[]{:S(2)}, u32[]{:S(2)}) %collective-permute-start.33) | collective-permute-done | bytes 393248 | tf_op jit(solution)/shard_map/ppermute | solution.py:855
  289.1 1.5 collective-permute-start.34
  290.7 2.6 spread_outer.2.refs_0_
  293.2 13.5 %collective-permute-done.34 = bf16[100,1152]{1,0:T(8,128)(2,1)S(1)} collective-permute-done((bf16[100,1152]{1,0:T(8,128)(2,1)S(1)}, bf16[100,1152]{1,0:T(8,128)(2,1)S(1)}, u32[]{:S(2)}, u32[]{:S(2)}) %collective-permute-start.34) | collective-permute-done | bytes 230432 | tf_op jit(solution)/shard_map/ppermute | solution.py:855
  312.8 4.2 %spread_inner.2 = (f32[768,3072]{1,0:T(8,128)}, f32[768,768]{1,0:T(8,128)}) custom-call(s32[1]{0:T(128)} %bitcast.16.at_ref, bf16[1280,768]{1,0:T(8,128)(2,1)S(1)} %pad_maximum_fusion.1.first_ref, bf16[768,768]{1,0:T(8,128)(2,1)S(1)} %pad_maximum_fusion.8.second_ref.third_ref, bf16[768,768]{1,0:T(8,128)(2,1)S(1)} %pad_maximum_fusion.8.second_ref.third_ref), custom_call_target="tpu_custom_call" | custom-call | flops 1048576 | bytes 1024 | tf_op jit(solution)/shard_map/spread_inner/pallas_call | solution.py:773
  317.0 2.6 spread_outer.3
  319.6 2.3 collective-permute-done.42
  323.6 6.2 %spread_inner.3 = (f32[768,3072]{1,0:T(8,128)}, f32[768,768]{1,0:T(8,128)}) custom-call(s32[1]{0:T(128)} %bitcast.19.at_ref, bf16[1280,768]{1,0:T(8,128)(2,1)} %collective-permute-done.40.first_ref, bf16[768,768]{1,0:T(8,128)(2,1)S(1)} %collective-permute-done.41.second_ref.third_ref, ...), custom_call_target="tpu_custom_call", output_to_operand_aliasing={{0}: (4, {}), {1}: (5, {})} | custom-call | flops 1048576 | bytes 1024 | tf_op jit(solution)/shard_map/spread_inner/pallas_call | solution.py:773
  331.4 4.3 %collective-permute-done.43 = bf16[400,1152]{1,0:T(8,128)(2,1)S(1)} collective-permute-done((bf16[400,1152]{1,0:T(8,128)(2,1)S(1)}, bf16[400,1152]{1,0:T(8,128)(2,1)S(1)}, u32[]{:S(2)}, u32[]{:S(2)}) %collective-permute-start.43) | collective-permute-done | bytes 921632 | tf_op jit(solution)/shard_map/ppermute | solution.py:855
  338.2 2.3 spread_columns.2
  343.1 4.1 %spread_columns.3 = (f32[768,768]{1,0:T(8,128)}, f32[768,768]{1,0:T(8,128)}, f32[768,768]{1,0:T(8,128)}) custom-call(s32[1]{0:T(128)} %bitcast.19.at_ref, bf16[800,1152]{1,0:T(8,128)(2,1)} %collective-permute-done.44.pool_ref, f32[768,768]{1,0:T(8,128)} %get-tuple-element.335.refs_0_, ...), custom_call_target="tpu_custom_call", output_to_operand_aliasing={{0}: (2, {}), {1}: (3, {}), {2}: (4, {})} | custom-call | flops 1048576 | bytes 1024 | tf_op jit(solution)/shard_map/spread_columns/pallas_call | solution.py:726
  (344 shorter events, 67.0 us)
Async XLA Ops:
  3.2 20.8 %collective-permute-start = (bf16[512,768]{1,0:T(8,128)(2,1)}, bf16[512,768]{1,0:T(8,128)(2,1)}, u32[]{:S(2)}, u32[]{:S(2)}) collective-permute-start(bf16[512,768]{1,0:T(8,128)(2,1)} %get-tuple-element.360), channel_id=1, source_target_pairs={{0,16},{1,17},{2,18},{3,19},{4,20},{5,21},{6,22},{7,23},{8,24},{9,... | collective-permute-start | bytes 2359304 | tf_op jit(solution)/shard_map/ppermute | solution.py:855
  6.1 18.5 %collective-permute-start.1 = (bf16[512,768]{1,0:T(8,128)(2,1)S(1)}, bf16[512,768]{1,0:T(8,128)(2,1)}, u32[]{:S(2)}, u32[]{:S(2)}) collective-permute-start(bf16[512,768]{1,0:T(8,128)(2,1)S(1)} %get-tuple-element.359), channel_id=1, source_target_pairs={{0,8},{8,0},{16,24},{24,16},{1,9},{9,1},{17,25},{25,17},{2,10},{10... | collective-permute-start | bytes 2359304 | tf_op jit(solution)/shard_map/ppermute | solution.py:844
  15.0 20.1 %copy-start.18 = (s32[32]{0:T(128)}, s32[32]{0:T(128)S(1)}, u32[]{:S(2)}) copy-start(s32[32]{0:T(128)S(1)} %pad_add_fusion.query_at_ref) | copy-start | bytes 388
  24.6 2.5 collective-permute-start.2
  33.3 16.4 %copy-start.20 = (bf16[2048,1152]{1,0:T(8,128)(2,1)}, bf16[2048,1152]{1,0:T(8,128)(2,1)S(1)}, u32[]{:S(2)}) copy-start(bf16[2048,1152]{1,0:T(8,128)(2,1)S(1)} %add_convert_fusion.q_ref.k_ref.v_ref) | copy-start | bytes 14155780
  33.3 19.7 %collective-permute-start.3 = (bf16[512,768]{1,0:T(8,128)(2,1)S(1)}, bf16[512,768]{1,0:T(8,128)(2,1)S(1)}, u32[]{:S(2)}, u32[]{:S(2)}) collective-permute-start(bf16[512,768]{1,0:T(8,128)(2,1)S(1)} %dynamic-slice_bitcast_fusion), channel_id=1, source_target_pairs={{0,16},{1,17},{2,18},{3,19},{4,20},{5,21},{6,22},{7,23},{8,24},{9,... | collective-permute-start | bytes 2359304 | tf_op jit(solution)/shard_map/ppermute | solution.py:855
  53.0 2.4 collective-permute-start.4
  113.2 9.1 %collective-permute-start.8 = (bf16[1536,768]{1,0:T(8,128)(2,1)}, bf16[1536,768]{1,0:T(8,128)(2,1)}, u32[]{:S(2)}, u32[]{:S(2)}) collective-permute-start(bf16[1536,768]{1,0:T(8,128)(2,1)} %tall_product.4), channel_id=1, source_target_pairs={{0,8},{8,0},{16,24},{24,16},{1,9},{9,1},{17,25},{25,17},{2,10},{10... | collective-permute-start | bytes 7077896 | tf_op jit(solution)/shard_map/ppermute | solution.py:844
  119.3 15.6 %collective-permute-start.5 = (bf16[1536,768]{1,0:T(8,128)(2,1)}, bf16[1536,768]{1,0:T(8,128)(2,1)}, u32[]{:S(2)}, u32[]{:S(2)}) collective-permute-start(bf16[1536,768]{1,0:T(8,128)(2,1)} %wide_product.2), channel_id=1, source_target_pairs={{0,8},{8,0},{16,24},{24,16},{1,9},{9,1},{17,25},{25,17},{2,10},{10... | collective-permute-start | bytes 7077896 | tf_op jit(solution)/shard_map/ppermute | solution.py:844
  122.1 12.8 %collective-permute-start.6 = (bf16[384,768]{1,0:T(8,128)(2,1)S(1)}, bf16[384,768]{1,0:T(8,128)(2,1)S(1)}, u32[]{:S(2)}, u32[]{:S(2)}) collective-permute-start(bf16[384,768]{1,0:T(8,128)(2,1)S(1)} %tall_product.5), channel_id=1, source_target_pairs={{0,8},{8,0},{16,24},{24,16},{1,9},{9,1},{17,25},{25,17},{2,10},{10... | collective-permute-start | bytes 1769480 | tf_op jit(solution)/shard_map/ppermute | solution.py:844
  130.7 13.4 %collective-permute-start.9 = (bf16[576,768]{1,0:T(8,128)(2,1)}, bf16[576,768]{1,0:T(8,128)(2,1)}, u32[]{:S(2)}, u32[]{:S(2)}) collective-permute-start(bf16[576,768]{1,0:T(8,128)(2,1)} %constant_dynamic-slice_fusion.10), channel_id=1, source_target_pairs={{0,16},{1,17},{2,18},{3,19},{4,20},{5,21},{6,22},{7,23},{8,9},{9,8... | collective-permute-start | bytes 2654216 | tf_op jit(solution)/shard_map/ppermute | solution.py:855
  133.1 1.8 collective-permute-start.7
  133.3 17.4 %collective-permute-start.11 = (bf16[1024,384]{1,0:T(8,128)(2,1)}, bf16[1024,384]{1,0:T(8,128)(2,1)S(1)}, u32[]{:S(2)}, u32[]{:S(2)}) collective-permute-start(bf16[1024,384]{1,0:T(8,128)(2,1)} %get-tuple-element.226), channel_id=1, source_target_pairs={{0,8},{8,0},{16,24},{24,16},{1,9},{9,1},{17,25},{25,17},{2,10},{10... | collective-permute-start | bytes 2359304 | tf_op jit(solution)/shard_map/ppermute | solution.py:844
  134.9 9.1 %collective-permute-start.10 = (bf16[192,768]{1,0:T(8,128)(2,1)S(1)}, bf16[192,768]{1,0:T(8,128)(2,1)S(1)}, u32[]{:S(2)}, u32[]{:S(2)}) collective-permute-start(bf16[192,768]{1,0:T(8,128)(2,1)S(1)} %constant_dynamic-slice_fusion.9), channel_id=1, source_target_pairs={{0,2},{1,3},{2,0},{3,1},{4,6},{5,7},{6,4},{7,5},{8,10},{9,11},{10,... | collective-permute-start | bytes 884744 | tf_op jit(solution)/shard_map/ppermute | solution.py:855
  147.2 16.4 %collective-permute-start.12 = (bf16[640,768]{1,0:T(8,128)(2,1)S(1)}, bf16[640,768]{1,0:T(8,128)(2,1)S(1)}, u32[]{:S(2)}, u32[]{:S(2)}) collective-permute-start(bf16[640,768]{1,0:T(8,128)(2,1)S(1)} %constant_dynamic-slice_fusion.8), channel_id=1, source_target_pairs={{0,16},{1,17},{2,18},{3,19},{4,20},{5,21},{6,22},{7,23},{8,9},{9,8... | collective-permute-start | bytes 2949128 | tf_op jit(solution)/shard_map/ppermute | solution.py:855
  149.0 14.6 %collective-permute-start.13 = (bf16[384,768]{1,0:T(8,128)(2,1)S(1)}, bf16[384,768]{1,0:T(8,128)(2,1)S(1)}, u32[]{:S(2)}, u32[]{:S(2)}) collective-permute-start(bf16[384,768]{1,0:T(8,128)(2,1)S(1)} %constant_dynamic-slice_fusion.7), channel_id=1, source_target_pairs={{0,2},{1,3},{2,0},{3,1},{4,6},{5,7},{6,4},{7,5},{8,10},{9,11},{10,... | collective-permute-start | bytes 1769480 | tf_op jit(solution)/shard_map/ppermute | solution.py:855
  164.3 14.3 %collective-permute-start.14 = (bf16[608,768]{1,0:T(8,128)(2,1)S(1)}, bf16[608,768]{1,0:T(8,128)(2,1)S(1)}, u32[]{:S(2)}, u32[]{:S(2)}) collective-permute-start(bf16[608,768]{1,0:T(8,128)(2,1)S(1)} %constant_dynamic-slice_fusion.6), channel_id=1, source_target_pairs={{0,1},{1,0},{2,3},{3,2},{4,5},{5,4},{6,7},{7,6},{8,10},{9,11},{10,... | collective-permute-start | bytes 2801672 | tf_op jit(solution)/shard_map/ppermute | solution.py:855
  165.4 13.2 %collective-permute-start.15 = (bf16[288,768]{1,0:T(8,128)(2,1)S(1)}, bf16[288,768]{1,0:T(8,128)(2,1)S(1)}, u32[]{:S(2)}, u32[]{:S(2)}) collective-permute-start(bf16[288,768]{1,0:T(8,128)(2,1)S(1)} %constant_dynamic-slice_fusion.5), channel_id=1, source_target_pairs={{0,16},{1,17},{2,18},{3,19},{4,20},{5,21},{6,22},{7,23},{8,24},{9,... | collective-permute-start | bytes 1327112 | tf_op jit(solution)/shard_map/ppermute | solution.py:855
  179.0 15.7 %collective-permute-start.16 = (bf16[304,768]{1,0:T(8,128)(2,1)S(1)}, bf16[304,768]{1,0:T(8,128)(2,1)S(1)}, u32[]{:S(2)}, u32[]{:S(2)}) collective-permute-start(bf16[304,768]{1,0:T(8,128)(2,1)S(1)} %constant_dynamic-slice_fusion.4), channel_id=1, source_target_pairs={{0,2},{1,3},{2,0},{3,1},{4,6},{5,7},{6,4},{7,5},{8,24},{9,25},{10,... | collective-permute-start | bytes 1400840 | tf_op jit(solution)/shard_map/ppermute | solution.py:855
  180.7 14.0 %collective-permute-start.17 = (bf16[144,768]{1,0:T(8,128)(2,1)S(1)}, bf16[144,768]{1,0:T(8,128)(2,1)S(1)}, u32[]{:S(2)}, u32[]{:S(2)}) collective-permute-start(bf16[144,768]{1,0:T(8,128)(2,1)S(1)} %constant_dynamic-slice_fusion.3), channel_id=1, source_target_pairs={{0,1},{1,0},{2,3},{3,2},{4,5},{5,4},{6,7},{7,6},{8,9},{9,8},{10,11... | collective-permute-start | bytes 663560 | tf_op jit(solution)/shard_map/ppermute | solution.py:855
  182.1 12.6 %collective-permute-start.18 = (bf16[256,768]{1,0:T(8,128)(2,1)S(1)}, bf16[256,768]{1,0:T(8,128)(2,1)S(1)}, u32[]{:S(2)}, u32[]{:S(2)}) collective-permute-start(bf16[256,768]{1,0:T(8,128)(2,1)S(1)} %copy-done.69), channel_id=1, source_target_pairs={{0,16},{1,17},{2,18},{3,19},{4,20},{5,21},{6,22},{7,23},{8,24},{9,... | collective-permute-start | bytes 1179656 | tf_op jit(solution)/shard_map/ppermute | solution.py:855
  194.9 14.8 %collective-permute-start.20 = (bf16[256,768]{1,0:T(8,128)(2,1)}, bf16[256,768]{1,0:T(8,128)(2,1)}, u32[]{:S(2)}, u32[]{:S(2)}) collective-permute-start(bf16[256,768]{1,0:T(8,128)(2,1)} %get-tuple-element.275), channel_id=1, source_target_pairs={{0,16},{1,17},{2,18},{3,19},{4,20},{5,21},{6,22},{7,23},{8,24},{9,... | collective-permute-start | bytes 1179656 | tf_op jit(solution)/shard_map/ppermute | solution.py:855
  196.4 12.5 %collective-permute-start.19 = (bf16[144,768]{1,0:T(8,128)(2,1)S(1)}, bf16[144,768]{1,0:T(8,128)(2,1)S(1)}, u32[]{:S(2)}, u32[]{:S(2)}) collective-permute-start(bf16[144,768]{1,0:T(8,128)(2,1)S(1)} %add_convert_fusion.15), channel_id=1, source_target_pairs={{0,4},{1,5},{2,6},{3,7},{4,0},{5,1},{6,2},{7,3},{8,12},{9,13},{10,... | collective-permute-start | bytes 663560 | tf_op jit(solution)/shard_map/ppermute | solution.py:855
  210.9 22.2 %collective-permute-start.22 = (bf16[400,1152]{1,0:T(8,128)(2,1)S(1)}, bf16[400,1152]{1,0:T(8,128)(2,1)S(1)}, u32[]{:S(2)}, u32[]{:S(2)}) collective-permute-start(bf16[400,1152]{1,0:T(8,128)(2,1)S(1)} %constant_dynamic-slice_fusion.2), channel_id=1, source_target_pairs={{0,16},{1,17},{2,18},{3,19},{4,20},{5,21},{6,22},{7,23},{8,9},{9,8... | collective-permute-start | bytes 2764808 | tf_op jit(solution)/shard_map/ppermute | solution.py:855
  211.7 21.4 %collective-permute-start.21 = (bf16[304,768]{1,0:T(8,128)(2,1)S(1)}, bf16[304,768]{1,0:T(8,128)(2,1)S(1)}, u32[]{:S(2)}, u32[]{:S(2)}) collective-permute-start(bf16[304,768]{1,0:T(8,128)(2,1)S(1)} %add_convert_fusion.8), channel_id=1, source_target_pairs={{0,4},{1,5},{2,6},{3,7},{4,0},{5,1},{6,2},{7,3},{8,12},{9,13},{10,... | collective-permute-start | bytes 1400840 | tf_op jit(solution)/shard_map/ppermute | solution.py:855
  221.0 26.9 %collective-permute-start.26 = (bf16[1024,768]{1,0:T(8,128)(2,1)}, bf16[1024,768]{1,0:T(8,128)(2,1)}, u32[]{:S(2)}, u32[]{:S(2)}) collective-permute-start(bf16[1024,768]{1,0:T(8,128)(2,1)} %get-tuple-element.287), channel_id=1, source_target_pairs={{0,8},{8,0},{16,24},{24,16},{1,9},{9,1},{17,25},{25,17},{2,10},{10... | collective-permute-start | bytes 4718600 | tf_op jit(solution)/shard_map/ppermute | solution.py:844
  234.6 13.3 %collective-permute-start.25 = (bf16[200,1152]{1,0:T(8,128)(2,1)S(1)}, bf16[200,1152]{1,0:T(8,128)(2,1)S(1)}, u32[]{:S(2)}, u32[]{:S(2)}) collective-permute-start(bf16[200,1152]{1,0:T(8,128)(2,1)S(1)} %constant_dynamic-slice_fusion.1), channel_id=1, source_target_pairs={{0,1},{1,0},{2,3},{3,2},{4,5},{5,4},{6,7},{7,6},{8,10},{9,11},{10,... | collective-permute-start | bytes 1382408 | tf_op jit(solution)/shard_map/ppermute | solution.py:855
  236.4 11.5 %collective-permute-start.23 = (bf16[304,768]{1,0:T(8,128)(2,1)S(1)}, bf16[304,768]{1,0:T(8,128)(2,1)S(1)}, u32[]{:S(2)}, u32[]{:S(2)}) collective-permute-start(bf16[304,768]{1,0:T(8,128)(2,1)S(1)} %add_convert_fusion.7), channel_id=1, source_target_pairs={{0,2},{1,3},{2,0},{3,1},{4,6},{5,7},{6,4},{7,5},{8,24},{9,25},{10,... | collective-permute-start | bytes 1400840 | tf_op jit(solution)/shard_map/ppermute | solution.py:855
  236.6 11.3 %collective-permute-start.24 = (bf16[144,768]{1,0:T(8,128)(2,1)S(1)}, bf16[144,768]{1,0:T(8,128)(2,1)S(1)}, u32[]{:S(2)}, u32[]{:S(2)}) collective-permute-start(bf16[144,768]{1,0:T(8,128)(2,1)S(1)} %add_convert_fusion.14), channel_id=1, source_target_pairs={{0,1},{1,0},{2,3},{3,2},{4,5},{5,4},{6,7},{7,6},{8,9},{9,8},{10,11... | collective-permute-start | bytes 663560 | tf_op jit(solution)/shard_map/ppermute | solution.py:855
  248.0 12.3 %collective-permute-start.28 = (bf16[288,768]{1,0:T(8,128)(2,1)S(1)}, bf16[288,768]{1,0:T(8,128)(2,1)S(1)}, u32[]{:S(2)}, u32[]{:S(2)}) collective-permute-start(bf16[288,768]{1,0:T(8,128)(2,1)S(1)} %pad_maximum_fusion.16), channel_id=1, source_target_pairs={{0,16},{1,17},{2,18},{3,19},{4,20},{5,21},{6,22},{7,23},{8,24},{9,... | collective-permute-start | bytes 1327112 | tf_op jit(solution)/shard_map/ppermute | solution.py:855
  249.5 13.6 %collective-permute-start.27 = (bf16[608,768]{1,0:T(8,128)(2,1)S(1)}, bf16[608,768]{1,0:T(8,128)(2,1)S(1)}, u32[]{:S(2)}, u32[]{:S(2)}) collective-permute-start(bf16[608,768]{1,0:T(8,128)(2,1)S(1)} %pad_maximum_fusion.10), channel_id=1, source_target_pairs={{0,1},{1,0},{2,3},{3,2},{4,5},{5,4},{6,7},{7,6},{8,10},{9,11},{10,... | collective-permute-start | bytes 2801672 | tf_op jit(solution)/shard_map/ppermute | solution.py:855
  251.4 8.8 %collective-permute-start.29 = (bf16[100,1152]{1,0:T(8,128)(2,1)S(1)}, bf16[100,1152]{1,0:T(8,128)(2,1)S(1)}, u32[]{:S(2)}, u32[]{:S(2)}) collective-permute-start(bf16[100,1152]{1,0:T(8,128)(2,1)S(1)} %constant_dynamic-slice_fusion), channel_id=1, source_target_pairs={{0,2},{1,3},{2,0},{3,1},{4,6},{5,7},{6,4},{7,5},{8,24},{9,25},{10,... | collective-permute-start | bytes 691208 | tf_op jit(solution)/shard_map/ppermute | solution.py:855
  263.6 22.3 %collective-permute-start.31 = (bf16[576,768]{1,0:T(8,128)(2,1)S(1)}, bf16[576,768]{1,0:T(8,128)(2,1)S(1)}, u32[]{:S(2)}, u32[]{:S(2)}) collective-permute-start(bf16[576,768]{1,0:T(8,128)(2,1)S(1)} %slice.151), channel_id=1, source_target_pairs={{0,16},{1,17},{2,18},{3,19},{4,20},{5,21},{6,22},{7,23},{8,9},{9,8... | collective-permute-start | bytes 2654216 | tf_op jit(solution)/shard_map/ppermute | solution.py:855
  264.6 14.7 %collective-permute-start.32 = (bf16[192,768]{1,0:T(8,128)(2,1)S(1)}, bf16[192,768]{1,0:T(8,128)(2,1)S(1)}, u32[]{:S(2)}, u32[]{:S(2)}) collective-permute-start(bf16[192,768]{1,0:T(8,128)(2,1)S(1)} %slice.152), channel_id=1, source_target_pairs={{0,2},{1,3},{2,0},{3,1},{4,6},{5,7},{6,4},{7,5},{8,10},{9,11},{10,... | collective-permute-start | bytes 884744 | tf_op jit(solution)/shard_map/ppermute | solution.py:855
  264.7 20.4 %collective-permute-start.33 = (bf16[256,768]{1,0:T(8,128)(2,1)S(1)}, bf16[256,768]{1,0:T(8,128)(2,1)S(1)}, u32[]{:S(2)}, u32[]{:S(2)}) collective-permute-start(bf16[256,768]{1,0:T(8,128)(2,1)S(1)} %slice.131), channel_id=1, source_target_pairs={{0,16},{1,17},{2,18},{3,19},{4,20},{5,21},{6,22},{7,23},{8,24},{9,... | collective-permute-start | bytes 1179656 | tf_op jit(solution)/shard_map/ppermute | solution.py:855
  266.2 13.1 %collective-permute-start.30 = (bf16[100,1152]{1,0:T(8,128)(2,1)S(1)}, bf16[100,1152]{1,0:T(8,128)(2,1)S(1)}, u32[]{:S(2)}, u32[]{:S(2)}) collective-permute-start(bf16[100,1152]{1,0:T(8,128)(2,1)S(1)} %add_convert_fusion.13), channel_id=1, source_target_pairs={{0,4},{1,5},{2,6},{3,7},{4,0},{5,1},{6,2},{7,3},{8,12},{9,13},{10,... | collective-permute-start | bytes 691208 | tf_op jit(solution)/shard_map/ppermute | solution.py:855
  286.2 20.5 %collective-permute-start.37 = (bf16[1152,768]{1,0:T(8,128)(2,1)S(1)}, bf16[1152,768]{1,0:T(8,128)(2,1)S(1)}, u32[]{:S(2)}, u32[]{:S(2)}) collective-permute-start(bf16[1152,768]{1,0:T(8,128)(2,1)S(1)} %pad_maximum_fusion.5.first_ref), channel_id=1, source_target_pairs={{0,8},{8,0},{16,24},{24,16},{1,9},{9,1},{17,25},{25,17},{2,10},{10... | collective-permute-start | bytes 5308424 | tf_op jit(solution)/shard_map/ppermute | solution.py:844
  286.4 20.4 %collective-permute-start.35 = (bf16[640,768]{1,0:T(8,128)(2,1)}, bf16[640,768]{1,0:T(8,128)(2,1)S(1)}, u32[]{:S(2)}, u32[]{:S(2)}) collective-permute-start(bf16[640,768]{1,0:T(8,128)(2,1)} %pad_maximum_fusion.9), channel_id=1, source_target_pairs={{0,16},{1,17},{2,18},{3,19},{4,20},{5,21},{6,22},{7,23},{8,9},{9,8... | collective-permute-start | bytes 2949128 | tf_op jit(solution)/shard_map/ppermute | solution.py:855
  288.3 18.4 %collective-permute-start.38 = (bf16[384,768]{1,0:T(8,128)(2,1)S(1)}, bf16[384,768]{1,0:T(8,128)(2,1)S(1)}, u32[]{:S(2)}, u32[]{:S(2)}) collective-permute-start(bf16[384,768]{1,0:T(8,128)(2,1)S(1)} %pad_maximum_fusion.14.second_ref), channel_id=1, source_target_pairs={{0,8},{8,0},{16,24},{24,16},{1,9},{9,1},{17,25},{25,17},{2,10},{10... | collective-permute-start | bytes 1769480 | tf_op jit(solution)/shard_map/ppermute | solution.py:844
  288.4 18.3 %collective-permute-start.36 = (bf16[384,768]{1,0:T(8,128)(2,1)S(1)}, bf16[384,768]{1,0:T(8,128)(2,1)S(1)}, u32[]{:S(2)}, u32[]{:S(2)}) collective-permute-start(bf16[384,768]{1,0:T(8,128)(2,1)S(1)} %copy-done.34), channel_id=1, source_target_pairs={{0,2},{1,3},{2,0},{3,1},{4,6},{5,7},{6,4},{7,5},{8,10},{9,11},{10,... | collective-permute-start | bytes 1769480 | tf_op jit(solution)/shard_map/ppermute | solution.py:855
  289.1 17.6 %copy-start.29 = (bf16[640,768]{1,0:T(8,128)(2,1)S(1)}, bf16[640,768]{1,0:T(8,128)(2,1)}, u32[]{:S(2)}) copy-start(bf16[640,768]{1,0:T(8,128)(2,1)} %pad_maximum_fusion.9) | copy-start | bytes 2949124
  289.1 17.6 %collective-permute-start.34 = (bf16[100,1152]{1,0:T(8,128)(2,1)S(1)}, bf16[100,1152]{1,0:T(8,128)(2,1)S(1)}, u32[]{:S(2)}, u32[]{:S(2)}) collective-permute-start(bf16[100,1152]{1,0:T(8,128)(2,1)S(1)} %add_convert_fusion.12), channel_id=1, source_target_pairs={{0,2},{1,3},{2,0},{3,1},{4,6},{5,7},{6,4},{7,5},{8,24},{9,25},{10,... | collective-permute-start | bytes 691208 | tf_op jit(solution)/shard_map/ppermute | solution.py:855
  308.5 13.4 %collective-permute-start.40 = (bf16[1280,768]{1,0:T(8,128)(2,1)S(1)}, bf16[1280,768]{1,0:T(8,128)(2,1)}, u32[]{:S(2)}, u32[]{:S(2)}) collective-permute-start(bf16[1280,768]{1,0:T(8,128)(2,1)S(1)} %pad_maximum_fusion.1.first_ref), channel_id=1, source_target_pairs={{0,8},{8,0},{16,24},{24,16},{1,9},{9,1},{17,25},{25,17},{2,10},{10... | collective-permute-start | bytes 5898248 | tf_op jit(solution)/shard_map/ppermute | solution.py:844
  309.8 12.1 %collective-permute-start.41 = (bf16[768,768]{1,0:T(8,128)(2,1)S(1)}, bf16[768,768]{1,0:T(8,128)(2,1)S(1)}, u32[]{:S(2)}, u32[]{:S(2)}) collective-permute-start(bf16[768,768]{1,0:T(8,128)(2,1)S(1)} %pad_maximum_fusion.8.second_ref.third_ref), channel_id=1, source_target_pairs={{0,8},{8,0},{16,24},{24,16},{1,9},{9,1},{17,25},{25,17},{2,10},{10... | collective-permute-start | bytes 3538952 | tf_op jit(solution)/shard_map/ppermute | solution.py:844
  310.8 11.1 %collective-permute-start.39 = (bf16[200,1152]{1,0:T(8,128)(2,1)S(1)}, bf16[200,1152]{1,0:T(8,128)(2,1)S(1)}, u32[]{:S(2)}, u32[]{:S(2)}) collective-permute-start(bf16[200,1152]{1,0:T(8,128)(2,1)S(1)} %pad_maximum_fusion.15), channel_id=1, source_target_pairs={{0,1},{1,0},{2,3},{3,2},{4,5},{5,4},{6,7},{7,6},{8,10},{9,11},{10,... | collective-permute-start | bytes 1382408 | tf_op jit(solution)/shard_map/ppermute | solution.py:855
  311.9 10.1 %collective-permute-start.42 = (bf16[256,768]{1,0:T(8,128)(2,1)S(1)}, bf16[256,768]{1,0:T(8,128)(2,1)S(1)}, u32[]{:S(2)}, u32[]{:S(2)}) collective-permute-start(bf16[256,768]{1,0:T(8,128)(2,1)S(1)} %slice.132), channel_id=1, source_target_pairs={{0,16},{1,17},{2,18},{3,19},{4,20},{5,21},{6,22},{7,23},{8,24},{9,... | collective-permute-start | bytes 1179656 | tf_op jit(solution)/shard_map/ppermute | solution.py:855
  322.2 13.5 %collective-permute-start.43 = (bf16[400,1152]{1,0:T(8,128)(2,1)S(1)}, bf16[400,1152]{1,0:T(8,128)(2,1)S(1)}, u32[]{:S(2)}, u32[]{:S(2)}) collective-permute-start(bf16[400,1152]{1,0:T(8,128)(2,1)S(1)} %pad_maximum_fusion.11), channel_id=1, source_target_pairs={{0,16},{1,17},{2,18},{3,19},{4,20},{5,21},{6,22},{7,23},{8,9},{9,8... | collective-permute-start | bytes 2764808 | tf_op jit(solution)/shard_map/ppermute | solution.py:855
  336.2 5.0 %collective-permute-start.44 = (bf16[800,1152]{1,0:T(8,128)(2,1)S(1)}, bf16[800,1152]{1,0:T(8,128)(2,1)}, u32[]{:S(2)}, u32[]{:S(2)}) collective-permute-start(bf16[800,1152]{1,0:T(8,128)(2,1)S(1)} %pad_maximum_fusion.3.pool_ref), channel_id=1, source_target_pairs={{0,8},{8,0},{16,24},{24,16},{1,9},{9,1},{17,25},{25,17},{2,10},{10... | collective-permute-start | bytes 5529608 | tf_op jit(solution)/shard_map/ppermute | solution.py:844
  (68 other events, 306.3 us)
